TPU v7x, 32 devices: a whole 2x2x4 slice. The times are simulated.
32 devices in a mesh: row: 4 (over z), col: 8 (over y, x, core).
Axes of the slice: x: 2, y: 2, z: 4, core: 2. Of those that a mesh axis runs over, the one named last changes fastest.
Arguments:
- v_coef: float32 [2, 512, 768, 256], P(None, 'col', 'row'), may hold values from -0.75 to 0.75
- vort_coef: float32 [2, 512, 768, 256], P(None, 'col', 'row'), may hold values from -6 to 6
- plane_ops: float32 [3, 12, 256], replicated, may hold values from -0.375 to 0.375
- inverse_ops: float32 [2, 256, 12], replicated, may hold values from -1.75 to 1.75
Outputs:
- vort_rhs: float32 [2, 512, 768, 256], P(None, 'col', 'row')
- lapv_rhs: float32 [2, 512, 768, 256], P(None, 'col', 'row')
All inputs are finite; a program needn't handle non-finite values.
Results may differ from a plain program's by a relative error of at most 0.00012.
Values sent between devices are 32-bit elements; how exact they have to be, the bound alone decides.
A program may use at most 192 MiB of HBM per device.

v0:
```python
import math

import jax
import jax.numpy as jnp
from jax import lax
from jax.sharding import PartitionSpec as P

PRECISE = lax.Precision.HIGHEST
STREAM_STEP = 0.25
SPAN_STEP = 2.0 / 3.0
INVERSE_SCALE = 1.0 / 32.0
FORWARD_SCALE = 32.0


def signed_modes(first, count, total):
    modes = first + jnp.arange(count, dtype=jnp.int32)
    return jnp.where(modes < total // 2, modes, modes - total)


def span_tables(total):
    points = 3 * total // 2
    signed = signed_modes(0, total, total)
    grid = jnp.arange(points, dtype=jnp.int32)
    phase = jnp.mod(signed[:, None] * grid[None, :], points).astype(jnp.float32)
    angle = phase * (2.0 * math.pi / points)
    cosine = jnp.cos(angle)
    sine = jnp.sin(angle)
    inverse = jnp.stack(
        [jnp.stack([cosine, sine], axis=1), jnp.stack([-sine, cosine], axis=1)], axis=0
    )
    factor = FORWARD_SCALE / points
    forward = (
        jnp.stack(
            [jnp.stack([cosine.T, -sine.T], axis=1), jnp.stack([sine.T, cosine.T], axis=1)], axis=0
        )
        * factor
    )
    return (inverse, forward)


def stream_tables(total):
    points = 3 * total
    modes = jnp.arange(total, dtype=jnp.int32)
    grid = jnp.arange(points, dtype=jnp.int32)
    phase = jnp.mod(modes[:, None] * grid[None, :], points).astype(jnp.float32)
    angle = phase * (2.0 * math.pi / points)
    cosine = jnp.cos(angle)
    sine = jnp.sin(angle)
    weights = jnp.where(modes == 0, 1.0, 2.0).astype(jnp.float32)[:, None]
    inverse = jnp.stack([weights * cosine, -weights * sine], axis=0) * INVERSE_SCALE
    forward = jnp.stack([cosine.T, -sine.T], axis=1) * (1.0 / points)
    return (inverse, forward)


def rotate(pair, factor):
    return (-factor * pair[1], factor * pair[0])


def combine(first, second, sign):
    return (first[0] + sign * second[0], first[1] + sign * second[1])


def scaled(pair, factor):
    return (pair[0] * factor, pair[1] * factor)


def split_pair(values):
    return (values[..., 0, :], values[..., 1, :])


def join_pair(pair):
    return jnp.stack(pair, axis=-2)


def build_fields(values, stream, span):
    v_base = split_pair(values[0])
    v_slope = split_pair(values[1])
    v_curve = split_pair(values[2])
    g_base = split_pair(values[3])
    g_slope = split_pair(values[4])
    square = stream * stream + span * span
    recip = 1.0 / jnp.where(square > 0, square, 1.0)
    along = scaled(combine(rotate(v_slope, stream), rotate(g_base, span), -1.0), recip)
    across = scaled(combine(rotate(v_slope, span), rotate(g_base, stream), 1.0), recip)
    omega_x = combine(
        scaled(combine(rotate(v_curve, span), rotate(g_slope, stream), 1.0), recip),
        rotate(v_base, span),
        -1.0,
    )
    omega_z = combine(
        rotate(v_base, stream),
        scaled(combine(rotate(v_curve, stream), rotate(g_slope, span), -1.0), recip),
        -1.0,
    )
    group_members = [along, v_base, across, omega_x, g_base, omega_z]
    return jnp.stack([join_pair(member) for member in group_members], axis=0)


def per_device(v_coef, vort_coef, plane_ops, inverse_ops):
    row_count = lax.axis_size("row")
    column_total_count = lax.axis_size("col")
    stream_local = v_coef.shape[1]
    span_local = v_coef.shape[2]
    stream_total = stream_local * column_total_count
    span_total = span_local * row_count
    stream_first = lax.axis_index("col") * stream_local
    span_first = lax.axis_index("row") * span_local
    stream_here = (
        STREAM_STEP * (stream_first + jnp.arange(stream_local, dtype=jnp.int32)).astype(jnp.float32)
    )[:, None]
    span_here = (SPAN_STEP * signed_modes(span_first, span_local, span_total).astype(jnp.float32))[
        None, :
    ]
    span_in, span_out = span_tables(span_total)
    stream_in, stream_out = stream_tables(stream_total)
    v_values = jnp.einsum("rpj,cxkj->rpxck", plane_ops, v_coef, precision=PRECISE)
    g_values = jnp.einsum("rpj,cxkj->rpxck", plane_ops[:2], vort_coef, precision=PRECISE)
    values = jnp.concatenate([v_values, g_values], axis=0)
    fields = build_fields(values, stream_here, span_here)
    pencils = lax.all_to_all(fields, "row", split_axis=1, concat_axis=4, tiled=True)
    span_phys = jnp.einsum("fpxck,ckdz->fpdxz", pencils, span_in, precision=PRECISE)
    arrived = lax.all_to_all(span_phys, "col", split_axis=4, concat_axis=3, tiled=True)
    physical = jnp.einsum("fpcmz,cmx->fpzx", arrived, stream_in, precision=PRECISE)
    velocity = physical[0:3]
    vorticity = physical[3:6]
    product_streamwise = velocity[1] * vorticity[2] - velocity[2] * vorticity[1]
    product_normal = velocity[2] * vorticity[0] - velocity[0] * vorticity[2]
    product_spanwise = velocity[0] * vorticity[1] - velocity[1] * vorticity[0]
    products = jnp.stack([product_streamwise, product_normal, product_spanwise], axis=0)
    stream_spec = jnp.einsum("fpzx,xcm->fpcmz", products, stream_out, precision=PRECISE)
    returned = lax.all_to_all(stream_spec, "col", split_axis=3, concat_axis=4, tiled=True)
    full_spec = jnp.einsum("fpdxz,dzck->fpxck", returned, span_out, precision=PRECISE)
    home = lax.all_to_all(full_spec, "row", split_axis=4, concat_axis=1, tiled=True)
    h_x = split_pair(home[0])
    h_y = split_pair(home[1])
    h_z = split_pair(home[2])
    square = stream_here * stream_here + span_here * span_here
    g_term = combine(rotate(h_x, span_here), rotate(h_z, stream_here), -1.0)
    s_term = scaled(combine(rotate(h_x, stream_here), rotate(h_z, span_here), 1.0), -1.0)
    y_term = scaled(h_y, -square)
    damp_g = 1.0 / jnp.sqrt(1.0 + square)
    damp_v = 1.0 / (1.0 + square)

    def contract(matrix, term):
        return jnp.einsum("jp,pxck->cxkj", matrix, join_pair(term), precision=PRECISE)

    vort_rhs = contract(inverse_ops[0], g_term) * damp_g[None, :, :, None]
    lapv_sum = contract(inverse_ops[1], s_term) + contract(inverse_ops[0], y_term)
    lapv_rhs = lapv_sum * damp_v[None, :, :, None]
    return (vort_rhs, lapv_rhs)


def solution(mesh):
    in_specs = (P(None, "col", "row", None), P(None, "col", "row", None), P(), P())
    out_specs = (P(None, "col", "row", None), P(None, "col", "row", None))
    return jax.shard_map(
        per_device, mesh=mesh, in_specs=in_specs, out_specs=out_specs, check_vma=False
    )
```

profile of v0, /device:TPU:8, one launch (start us, length us, event | category | flops | bytes accessed | tf_op | source)
XLA Modules:
  0.0 1262.4 jit_solution(10709031613174032278)
XLA Ops:
  0.7 28.1 %fusion.55 = f32[3,12,64,2,192]{4,1,0,2,3:T(8,128)S(1)} fusion(f32[2,64,192,256]{3,2,1,0:T(8,128)} %param.4, f32[3,12,256]{2,1,0:T(8,128)} %param.6), kind=kOutput, calls=%fused_computation.77 | convolution fusion | flops 2717908992 | bytes 28741632 | tf_op jit(solution)/shard_map/rpj,cxkj->rpxck/dot_general | solution.py:116
  28.8 3.2 slice_bitcast_fusion.1
  32.0 26.8 %fusion.61 = f32[2,12,64,2,192]{4,1,2,3,0:T(8,128)S(1)} fusion(f32[2,64,192,256]{3,2,1,0:T(8,128)} %param.5, f32[3,12,256]{2,1,0:T(8,128)S(1)} %copy-done.6), kind=kOutput, calls=%fused_computation.82 | convolution fusion | flops 1811939328 | bytes 27557888 | tf_op jit(solution)/shard_map/rpj,cxkj->rpxck/dot_general | solution.py:117
  58.8 0.4 slice_bitcast_fusion
  59.3 0.8 add_negate_fusion
  60.0 0.7 add_multiply_fusion.1
  60.8 1.6 fusion.64
  62.3 1.5 bitcast_dynamic-update-slice_fusion
  63.8 1.5 fusion.65
  65.4 0.6 copy-done.1
  66.0 1.1 multiply_add_fusion.1
  67.1 1.5 fusion.66
  68.6 1.5 slice_dynamic-update-slice_fusion
  70.1 1.5 fusion.67
  71.6 13.8 %copy.105 = f32[6,12,64,2,192]{4,2,3,0,1:T(8,128)} copy(f32[6,12,64,2,192]{4,1,2,3,0:T(8,128)} %fusion.67) | data formatting | bytes 14155776 | tf_op jit(solution)/shard_map/stack | solution.py:96
  85.4 6.2 all-to-all-start
  91.7 14.7 %fusion.38 = (f32[768,1,1152]{2,0,1:T(8,128)S(1)}, f32[768,1,1152]{2,0,1:T(8,128)S(1)}, f32[768,1,1152]{2,0,1:T(8,128)S(1)}) fusion(s32[768]{0:T(1024)S(1)} %compare_select_fusion.1), kind=kLoop, calls=%fused_computation.55 | loop fusion | flops 8847360 | bytes 10619904 | tf_op jit(solution)/shard_map/sin | solution.py:27
  106.3 5.6 maximum_bitcast_fusion.4
  112.0 182.4 %all-to-all-done = f32[6,12,64,2,192]{4,2,3,0,1:T(8,128)} async-done(((f32[6,12,64,2,192]{4,2,3,0,1:T(8,128)}), f32[6,12,64,2,192]{4,2,3,0,1:T(8,128)}, u32[]{:S(2)}, u32[]{:S(2)}) %all-to-all-start) | async-done | bytes 7077920 | tf_op jit(solution)/shard_map/all_to_all | solution.py:120
  294.4 15.7 %copy.107 = f32[6,3,64,2,4,192]{5,4,2,3,1,0:T(4,128)} copy(f32[6,3,64,2,4,192]{5,2,3,0,1,4:T(8,128)} %bitcast.27) | data formatting | bytes 14155776 | tf_op jit(solution)/shard_map/all_to_all | solution.py:120
  310.1 10.8 reshape.557
  320.9 57.5 %fusion.18 = f32[6,3,2,64,1152]{4,3,1,0,2:T(8,128)} fusion(f32[6,3,64,2,768,1]{4,2,3,1,0,5:T(8,128)} %reshape.557, f32[1,768,2,1152]{3,1,0,2:T(8,128)} %get-tuple-element.36, f32[1,768,2,1152]{3,1,0,2:T(8,128)} %get-tuple-element.35), kind=kOutput, calls=%fused_computation.29 | convolution fusion | flops 48925900800 | bytes 31850496 | tf_op jit(solution)/shard_map/fpxck,ckdz->fpdxz/dot_general | solution.py:121
  378.3 27.2 %copy.108 = f32[6,3,2,64,1152]{3,2,1,0,4:T(2,128)} copy(f32[6,3,2,64,1152]{4,3,1,0,2:T(8,128)} %fusion.18) | data formatting | bytes 21233664 | tf_op jit(solution)/shard_map/fpxck,ckdz->fpdxz/transpose | solution.py:121
  405.6 25.0 %reshape.570 = f32[8,1,331776]{2,1,0:T(1,128)} reshape(f32[1152,6,3,2,64]{4,3,2,1,0:T(2,128)} %bitcast.176) | data formatting | bytes 21233664
  430.6 5.6 all-to-all-start.1
  436.2 13.7 %sine_negate_fusion = (f32[1536,1,512]{2,0,1:T(8,128)S(1)}, f32[1536,1,512]{2,0,1:T(8,128)}) fusion(), kind=kLoop, calls=%fused_computation.70 | loop fusion | flops 7864320 | bytes 6291456 | tf_op jit(solution)/shard_map/neg | solution.py:51
  449.9 14.1 %sine_multiply_fusion = (f32[1,512,1536]{2,1,0:T(8,128)}, f32[1,512,1536]{2,1,0:T(8,128)}) fusion(f32[512]{0:T(512)S(1)} %fusion.98, f32[512]{0:T(512)S(1)} %fusion.95), kind=kLoop, calls=%fused_computation.64 | loop fusion | flops 8650752 | bytes 6295552 | tf_op jit(solution)/shard_map/mul | solution.py:50
  464.0 90.1 %all-to-all-done.1 = f32[8,1,331776]{2,1,0:T(1,128)} async-done(((f32[8,1,331776]{2,1,0:T(1,128)}), f32[8,1,331776]{2,1,0:T(1,128)}, u32[]{:S(2)}, u32[]{:S(2)}) %all-to-all-start.1) | async-done | bytes 10616864 | tf_op jit(solution)/shard_map/all_to_all | solution.py:122
  554.1 0.5 broadcast.713
  554.7 101.6 %reduce = f32[8,331776]{1,0:T(8,128)} reduce(f32[8,1,331776]{2,1,0:T(1,128)} %all-to-all-done.1, f32[]{:T(128)} %broadcast.713), dimensions={1}, to_apply=%all_to_all.54.reduce_sub_computation | reduce | bytes 21233668 | tf_op jit(solution)/shard_map/all_to_all | solution.py:122
  656.3 36.6 %reshape.571 = f32[1152,6,3,2,64]{4,3,2,1,0:T(2,128)} reshape(f32[8,331776]{1,0:T(8,128)} %reduce) | data formatting | bytes 21233664
  692.9 17.8 %copy.204 = f32[6,3,2,64,8,144]{3,4,5,2,1,0:T(8,128)} copy(f32[6,3,2,64,8,144]{3,2,1,0,5,4:T(2,128)} %bitcast.177) | data formatting | bytes 21233664 | tf_op jit(solution)/shard_map/all_to_all | solution.py:122
  710.7 18.3 %all_to_all.57 = f32[6,3,2,512,144]{3,4,2,1,0:T(8,128)} reshape(f32[6,3,2,8,64,144]{4,3,5,2,1,0:T(8,128)} %bitcast.178) | data formatting | bytes 21233664 | tf_op jit(solution)/shard_map/all_to_all | solution.py:122
  729.0 56.0 %convolution_bitcast_fusion = f32[6,3,144,1536]{3,2,1,0:T(8,128)S(1)} fusion(f32[6,3,2,512,144]{3,4,2,1,0:T(8,128)} %all_to_all.57, f32[1,512,1536]{2,1,0:T(8,128)} %get-tuple-element.67, f32[1,512,1536]{2,1,0:T(8,128)} %get-tuple-element.68), kind=kOutput, calls=%fused_computation.23 | convolution fusion | flops 48925507584 | bytes 32833536 | tf_op jit(solution)/shard_map/fpcmz,cmx->fpzx/dot_general | solution.py:123
  785.0 2.9 multiply_subtract_fusion.2
  787.9 29.1 %fusion.58 = f32[3,3,2,512,144]{3,4,1,0,2:T(8,128)} fusion(f32[1,3,144,1536]{3,2,1,0:T(8,128)} %get-tuple-element.14, f32[1,3,144,1536]{3,2,1,0:T(8,128)S(1)} %get-tuple-element.13, f32[1,3,144,1536]{3,2,1,0:T(8,128)S(1)} %get-tuple-element.12, f32[1536,1,512]{2,0,1:T(8,128)S(1)} %get-tuple-element.69, f32[1536,1,512]{2,0,1:T(8,128)S(1)} %copy-done.2), kind=kOutput, calls=%fused_computation.81 | convolution fusion | flops 24468307968 | bytes 19562496 | tf_op jit(solution)/shard_map/fpzx,xcm->fpcmz/dot_general | solution.py:130
  816.9 13.7 %copy.110 = f32[3,3,2,512,144]{4,2,1,0,3:T(2,128)} copy(f32[3,3,2,512,144]{3,4,1,0,2:T(8,128)} %fusion.58) | data formatting | bytes 10616832 | tf_op jit(solution)/shard_map/fpzx,xcm->fpcmz/transpose | solution.py:130
  830.6 5.1 all-to-all-start.2
  835.7 14.4 %fusion.80 = (f32[1152,1,768]{2,0,1:T(8,128)S(1)}, f32[1152,1,768]{2,0,1:T(8,128)S(1)}, f32[1152,1,768]{2,0,1:T(8,128)S(1)}) fusion(s32[768]{0:T(1024)S(1)} %compare_select_fusion.1), kind=kLoop, calls=%fused_computation.108 | loop fusion | flops 8847360 | bytes 10619904 | tf_op jit(solution)/shard_map/neg | solution.py:34
  850.1 5.8 maximum_bitcast_fusion.6
  855.9 85.1 %all-to-all-done.2 = f32[3,3,2,512,144]{4,2,1,0,3:T(2,128)} async-done(((f32[3,3,2,512,144]{4,2,1,0,3:T(2,128)}), f32[3,3,2,512,144]{4,2,1,0,3:T(2,128)}, u32[]{:S(2)}, u32[]{:S(2)}) %all-to-all-start.2) | async-done | bytes 5308448 | tf_op jit(solution)/shard_map/all_to_all | solution.py:131
  941.0 12.9 %copy.205 = f32[3,3,2,8,64,144]{5,3,4,2,1,0:T(8,128)} copy(f32[3,3,2,8,64,144]{5,2,1,0,4,3:T(2,128)} %bitcast.39) | data formatting | bytes 10616832 | tf_op jit(solution)/shard_map/all_to_all | solution.py:131
  953.9 9.8 reshape.563
  963.7 30.3 %fusion.74 = f32[3,3,64,2,768]{4,2,3,1,0:T(8,128)S(1)} fusion(f32[1,1152,2,768]{3,1,0,2:T(8,128)} %get-tuple-element.38, f32[1,1152,2,768]{3,1,0,2:T(8,128)} %get-tuple-element.37, f32[3,3,2,64,1152,1]{4,3,2,1,0,5:T(8,128)} %reshape.563), kind=kOutput, calls=%fused_computation.103 | convolution fusion | flops 24468258816 | bytes 23003136 | tf_op jit(solution)/shard_map/fpdxz,dzck->fpxck/dot_general | solution.py:132
  994.0 8.6 copy.114
  1002.6 9.8 reshape.572
  1012.4 7.4 all-to-all-start.3
  1019.9 1.4 fusion.115
  1021.3 71.7 %all-to-all-done.3 = f32[4,1,221184]{2,1,0:T(1,128)S(1)} async-done(((f32[4,1,221184]{2,1,0:T(1,128)}), f32[4,1,221184]{2,1,0:T(1,128)S(1)}, u32[]{:S(2)}, u32[]{:S(2)}) %all-to-all-start.3) | async-done | bytes 3538976 | tf_op jit(solution)/shard_map/all_to_all | solution.py:133
  1093.0 32.6 %reduce.1 = f32[4,221184]{1,0:T(4,128)} reduce(f32[4,1,221184]{2,1,0:T(1,128)S(1)} %all-to-all-done.3, f32[]{:T(128)} %broadcast.713), dimensions={1}, to_apply=%all_to_all.62.reduce_sub_computation | reduce | bytes 7077892 | tf_op jit(solution)/shard_map/all_to_all | solution.py:133
  1125.6 10.5 reshape.573
  1136.1 14.0 %copy.148 = f32[3,3,64,2,4,192]{5,4,2,3,1,0:T(4,128)} copy(f32[3,3,64,2,4,192]{2,3,1,0,5,4:T(2,128)} %bitcast.181) | data formatting | bytes 7077888 | tf_op jit(solution)/shard_map/all_to_all | solution.py:133
  1150.2 3.2 fusion.111
  1153.3 0.3 copy.126
  1153.8 0.3 copy.118
  1154.2 0.3 copy.116
  1154.9 1.1 fusion.83
  1156.0 1.1 fusion.87
  1157.1 0.9 copy_multiply_fusion.9
  1158.1 23.3 %fusion.71 = f32[64,2,192,256]{3,2,1,0:T(8,128)} fusion(f32[1,256,12]{1,0,2:T(1,128)S(1)} %copy-done.7, f32[12,64,1,192]{3,0,1,2:T(8,128)S(1)} %get-tuple-element.41, f32[12,64,1,192]{3,0,1,2:T(8,128)S(1)} %get-tuple-element.39), kind=kOutput, calls=%fused_computation.100 | convolution fusion | flops 906264576 | bytes 26357760 | tf_op jit(solution)/shard_map/jp,pxck->cxkj/dot_general | solution.py:145
  1181.4 29.9 %multiply_bitcast_fusion = f32[2,64,192,256]{3,2,0,1:T(8,128)} fusion(f32[64,2,192,256]{3,2,1,0:T(8,128)} %fusion.71, f32[64,192]{1,0:T(8,128)S(1)} %copy-done.4, f32[12,64,1,192]{3,0,2,1:T(8,128)S(1)} %get-tuple-element.50, f32[12,64,1,192]{3,0,2,1:T(8,128)S(1)} %get-tuple-element.49, f32[1,256,12]{1,0,2:T(1,128)S(1)} %get-tuple-element.52), kind=kOutput, calls=%fused_computation.4 | convolution fusion | flops 918847488 | bytes 51572736 | tf_op jit(solution)/shard_map/jp,pxck->cxkj/dot_general | solution.py:145
  1211.3 17.6 %copy.130 = f32[2,64,192,256]{3,2,1,0:T(8,128)} copy(f32[2,64,192,256]{3,2,0,1:T(8,128)} %multiply_bitcast_fusion) | data formatting | bytes 50331648
  1228.9 24.5 %multiply_bitcast_fusion.1 = f32[2,64,192,256]{3,2,0,1:T(8,128)S(1)} fusion(f32[64,192]{1,0:T(8,128)S(1)} %copy-done.3, f32[1,256,12]{1,0,2:T(1,128)S(1)} %get-tuple-element.52, f32[12,64,1,192]{3,0,1,2:T(8,128)S(1)} %get-tuple-element.42, f32[12,64,1,192]{3,0,1,2:T(8,128)S(1)} %get-tuple-element.40), kind=kOutput, calls=%fused_computation.5 | convolution fusion | flops 912556032 | bytes 26406912 | tf_op jit(solution)/shard_map/jp,pxck->cxkj/dot_general | solution.py:145
  1253.4 8.8 copy.129
  (41 shorter events, 0.6 us)
Async XLA Ops:
  0.6 64.7 %copy-start.8 = (f32[192]{0:T(256)}, f32[192]{0:T(256)S(1)}, u32[]{:S(2)}) copy-start(f32[192]{0:T(256)S(1)} %get-tuple-element.63) | copy-start | bytes 2308
  0.7 64.7 %copy-start.10 = (f32[192]{0:T(256)}, f32[192]{0:T(256)S(1)}, u32[]{:S(2)}) copy-start(f32[192]{0:T(256)S(1)} %fusion.100) | copy-start | bytes 2308
  0.7 64.7 %copy-start.12 = (f32[64]{0:T(128)}, f32[64]{0:T(128)S(1)}, u32[]{:S(2)}) copy-start(f32[64]{0:T(128)S(1)} %get-tuple-element.65) | copy-start | bytes 772
  0.7 64.7 %copy-start.14 = (f32[64]{0:T(128)}, f32[64]{0:T(128)S(1)}, u32[]{:S(2)}) copy-start(f32[64]{0:T(128)S(1)} %fusion.110) | copy-start | bytes 772
  28.8 3.2 copy-start.6
  62.3 3.1 copy-start
  62.3 3.7 copy-start.1
  85.4 209.0 %all-to-all-start = ((f32[6,12,64,2,192]{4,2,3,0,1:T(8,128)}), f32[6,12,64,2,192]{4,2,3,0,1:T(8,128)}, u32[]{:S(2)}, u32[]{:S(2)}) async-start(f32[6,12,64,2,192]{4,2,3,0,1:T(8,128)} %copy.105), calls=%async_computation | async-start | bytes 18874368 | tf_op jit(solution)/shard_map/all_to_all | solution.py:120
  430.6 123.5 %all-to-all-start.1 = ((f32[8,1,331776]{2,1,0:T(1,128)}), f32[8,1,331776]{2,1,0:T(1,128)}, u32[]{:S(2)}, u32[]{:S(2)}) async-start(f32[8,1,331776]{2,1,0:T(1,128)} %reshape.570), calls=%async_computation.1 | async-start | bytes 21233664 | tf_op jit(solution)/shard_map/all_to_all | solution.py:122
  785.0 2.9 copy-start.2
  830.6 110.4 %all-to-all-start.2 = ((f32[3,3,2,512,144]{4,2,1,0,3:T(2,128)}), f32[3,3,2,512,144]{4,2,1,0,3:T(2,128)}, u32[]{:S(2)}, u32[]{:S(2)}) async-start(f32[3,3,2,512,144]{4,2,1,0,3:T(2,128)} %copy.110), calls=%async_computation.2 | async-start | bytes 18874368 | tf_op jit(solution)/shard_map/all_to_all | solution.py:131
  1012.4 80.6 %all-to-all-start.3 = ((f32[4,1,221184]{2,1,0:T(1,128)}), f32[4,1,221184]{2,1,0:T(1,128)S(1)}, u32[]{:S(2)}, u32[]{:S(2)}) async-start(f32[4,1,221184]{2,1,0:T(1,128)} %reshape.572), calls=%async_computation.3 | async-start | bytes 7077888 | tf_op jit(solution)/shard_map/all_to_all | solution.py:133
  1154.2 0.7 copy-start.11
  1154.2 0.7 copy-start.15
  1154.5 1.4 copy-start.9
  1154.5 1.4 copy-start.13
  1154.9 2.2 copy-start.5
  1156.0 2.1 copy-start.7
  1158.0 23.3 %copy-start.4 = (f32[64,192]{1,0:T(8,128)S(1)}, f32[64,192]{1,0:T(8,128)}, u32[]{:S(2)}) copy-start(f32[64,192]{1,0:T(8,128)} %get-tuple-element.62) | copy-start | bytes 147460
  1211.3 17.6 %copy-start.3 = (f32[64,192]{1,0:T(8,128)S(1)}, f32[64,192]{1,0:T(8,128)}, u32[]{:S(2)}) copy-start(f32[64,192]{1,0:T(8,128)} %get-tuple-element.60) | copy-start | bytes 147460
where the time goes:
time: 1280 us; the launch traced here: 1260 us
  waiting for transfers between devices  429 us (34%)
  matrix products  305 us (24%)
  local copies, waits for them, and re-layouts  285 us (22%)
  other arithmetic  217 us (17%)
  starting transfers between devices  24.3 us (2%)
    all_to_all x1, waiting for transfers between devices, per_device(): lax.all_to_all(fields, 'row', split_axis=1, concat_axis=4, tiled=True)  182 us
    unnamed x40, local copies, waits for them, and re-layouts  112 us
    all_to_all x1, other arithmetic, per_device(): lax.all_to_all(span_phys, 'col', split_axis=4, concat_axis=3, tiled=True)  102 us
    all_to_all x1, waiting for transfers between devices, per_device(): lax.all_to_all(span_phys, 'col', split_axis=4, concat_axis=3, tiled=True)  90.1 us
    all_to_all x1, waiting for transfers between devices, per_device(): lax.all_to_all(stream_spec, 'col', split_axis=3, concat_axis=4, tiled=True)  85.1 us
    dot_general x3, matrix products, contract(): jnp.einsum('jp,pxck->cxkj', matrix, join_pair(term), precision=PRECISE)  77.8 us
    all_to_all x1, waiting for transfers between devices, per_device(): lax.all_to_all(full_spec, 'row', split_axis=4, concat_axis=1, tiled=True)  71.7 us
    dot_general x1, matrix products, per_device(): jnp.einsum('fpxck,ckdz->fpdxz', pencils, span_in, precision=PRECISE)  57.5 us
  transfers between devices with their start and end apart: 4, of which 4 were waited for; matrix products, arithmetic and copies ran while one was open for 6% of the time, Pallas kernels for 0%

commit v1 on v0

--- a/solution.py
+++ b/solution.py
@@ -1,8 +1,13 @@
+import functools
 import math
 
 import jax
 import jax.numpy as jnp
+import ml_dtypes
+import numpy as np
 from jax import lax
+from jax.experimental import pallas as pl
+from jax.experimental.pallas import tpu as pltpu
 from jax.sharding import PartitionSpec as P
 
 PRECISE = lax.Precision.HIGHEST
@@ -10,6 +15,497 @@
 SPAN_STEP = 2.0 / 3.0
 INVERSE_SCALE = 1.0 / 32.0
 FORWARD_SCALE = 32.0
+LANES = 128
+VMEM_LIMIT = 44 * 1024 * 1024
+MESH = pl.DeviceIdType.MESH
+F32 = jnp.float32
+BF16 = jnp.bfloat16
+
+
+def halves(table):
+    table = np.asarray(table, np.float32)
+    high = table.astype(ml_dtypes.bfloat16)
+    low = (table - high.astype(np.float32)).astype(ml_dtypes.bfloat16)
+    return np.stack([high, low], axis=0)
+
+
+def signed_order(rows, span_local, span_total):
+    n = (
+        span_local * np.arange(rows)[:, None, None]
+        + np.arange(2)[None, :, None]
+        + 2 * np.arange(span_local // 2)[None, None, :]
+    )
+    return np.where(n < span_total // 2, n, n - span_total)
+
+
+def span_fast_tables(rows, span_local, span_total):
+    points = 3 * span_total // 2
+    signed = signed_order(rows, span_local, span_total)
+    grid = np.arange(points // 2)
+    inverse, forward = [], []
+    for parity in range(2):
+        s = signed[:, parity, :].reshape(-1)
+        angle = np.mod(s[None, :] * grid[:, None], points) * (2.0 * math.pi / points)
+        inverse.append(np.concatenate([np.cos(angle), np.sin(angle)], axis=1))
+        factor = FORWARD_SCALE / points
+        forward.append(np.concatenate([np.cos(angle).T, np.sin(angle).T], axis=1) * factor)
+    return halves(np.stack(inverse)), halves(np.stack(forward))
+
+
+def stream_fast_tables(total):
+    points = 3 * total
+    grid = np.arange(points // 4) + 0.5
+    inverse, forward = [], []
+    for part in range(2):
+        for parity in range(2):
+            m = 2 * np.arange(total // 2) + parity
+            angle = np.mod(m[:, None] * grid[None, :], points) * (2.0 * math.pi / points)
+            wave = np.cos(angle) if part == 0 else -np.sin(angle)
+            weight = np.where(m == 0, 1.0, 2.0)[:, None]
+            inverse.append(weight * wave * INVERSE_SCALE)
+            forward.append(wave.T / points)
+    return halves(np.stack(inverse)), halves(np.stack(forward))
+
+
+def split(values):
+    high = values.astype(BF16)
+    return high, (values - high.astype(F32)).astype(BF16)
+
+
+def dot(a, b):
+    return jnp.dot(a, b, preferred_element_type=F32)
+
+
+def dot3(a_high, a_low, b_high, b_low):
+    return dot(a_high, b_high) + (dot(a_high, b_low) + dot(a_low, b_high))
+
+
+def times_i(values):
+    axis = values.ndim - 1
+    lane = lax.broadcasted_iota(jnp.int32, values.shape, axis)
+    turned = pltpu.roll(values, LANES // 2, axis)
+    return jnp.where(lane < LANES // 2, -turned, turned)
+
+
+def block_transpose(a):
+    lane = lax.broadcasted_iota(jnp.int32, a[0].shape, 1)
+    left = lane < 64
+    odd = (lane // 32) % 2 == 1
+    t = [None] * 4
+    for s in range(2):
+        t[s] = jnp.where(left, a[s], pltpu.roll(a[s + 2], 64, 1))
+        t[s + 2] = jnp.where(left, pltpu.roll(a[s], 64, 1), a[s + 2])
+    out = [None] * 4
+    for s in (0, 2):
+        out[s] = jnp.where(odd, pltpu.roll(t[s + 1], 32, 1), t[s])
+        out[s + 1] = jnp.where(odd, t[s + 1], pltpu.roll(t[s], 96, 1))
+    return out
+
+
+def contract_last(a, b):
+    return lax.dot_general(a, b, (((1,), (1,)), ((), ())), preferred_element_type=F32)
+
+
+def plane_kernel(v0, v1, g0, g1, wv_ref, wg_ref, out_ref, *, count):
+    flat = out_ref.reshape(out_ref.shape[0] * 16, LANES)
+    base = 0
+    for low_ref, high_ref, w_ref, ops in ((v0, v1, wv_ref, 3), (g0, g1, wg_ref, 2)):
+        refs = [ref.reshape(2 * 64 * 16, LANES) for ref in (low_ref, high_ref)]
+        pad = w_ref.shape[0] // 2
+        for parity in range(2):
+            for pair in range(4):
+                rows = []
+                for half in (2 * pair, 2 * pair + 1):
+                    for part in range(2):
+                        for odd in range(2):
+                            start = part * 1024 + odd * 16 + 2 * half + parity
+                            rows.append(
+                                jnp.concatenate(
+                                    [ref[pl.ds(start, 32, stride=32), :] for ref in refs], axis=1
+                                )
+                            )
+                high, low = split(jnp.concatenate(rows, axis=0))
+                first = contract_last(w_ref[...], high)
+                second = contract_last(w_ref[:pad], low)
+                sums = first[:pad] + (first[pad:] + second)
+                used = ops * count
+                for side in range(2):
+                    at = base * 16 + parity * 8 + 2 * pair + side
+                    flat[pl.ds(at, used, stride=16), :] = sums[
+                        :used, side * LANES : (side + 1) * LANES
+                    ]
+        base += ops * count
+
+
+def span_inverse_kernel(r_ref, kx_ref, kz_ref, t_ref, out_ref, high_ref, low_ref, *, rows, half):
+    modes = rows * half
+
+    @pl.when(pl.program_id(0) == 0)
+    def _():
+        kx = kx_ref[...]
+        for row in range(rows):
+            for parity in range(2):
+                kz = kz_ref[row, parity]
+                square = kx * kx + kz * kz
+                recip = 1.0 / jnp.where(square > 0, square, 1.0)
+                vb, vd, vdd, gb, gd = [r_ref[row, f, parity] for f in range(5)]
+                members = [
+                    times_i((kx * vd - kz * gb) * recip),
+                    vb,
+                    times_i((kz * vd + kx * gb) * recip),
+                    times_i((kz * vdd + kx * gd) * recip - kz * vb),
+                    gb,
+                    times_i(kx * vb - (kx * vdd - kz * gd) * recip),
+                ]
+                for f, member in enumerate(members):
+                    for place, values in ((0, member), (modes, times_i(member))):
+                        high, low = split(values)
+                        at = pl.ds(place + row * half, half)
+                        high_ref[f // 2, parity, at, pl.ds((f % 2) * LANES, LANES)] = high
+                        low_ref[f // 2, parity, at, pl.ds((f % 2) * LANES, LANES)] = low
+
+    pair = pl.program_id(0)
+    even, odd = [
+        dot3(t_ref[0, q], t_ref[1, q], high_ref[pair, q], low_ref[pair, q]) for q in range(2)
+    ]
+    plus, minus = even + odd, even - odd
+    dests = out_ref.shape[0]
+    step = out_ref.shape[2] // 2
+    for d in range(dests):
+        for f in range(2):
+            lanes = slice(f * LANES, (f + 1) * LANES)
+            out_ref[d, f, :step] = plus[d * step : (d + 1) * step, lanes]
+            out_ref[d, f, step:] = minus[d * step : (d + 1) * step, lanes]
+
+
+def stream_kernel(x_ref, ti_ref, tf_ref, out_ref):
+    sources, fields, block, _ = x_ref.shape
+    width = ti_ref.shape[3]
+    parts = [x_ref[s].reshape(fields * block, LANES) for s in range(sources)]
+    groups = [[] for _ in range(4)]
+    for s in range(0, sources, 4):
+        for g, piece in enumerate(block_transpose(parts[s : s + 4])):
+            groups[g].append(piece)
+    spectral = []
+    for g in range(4):
+        high, low = split(jnp.concatenate(groups[g], axis=1))
+        spectral.append(dot3(high, low, ti_ref[0, g], ti_ref[1, g]))
+    ce, co, se, so = [s.reshape(fields, block, width) for s in spectral]
+    a, b, c, d = ce + co, se + so, ce - co, se - so
+    products = []
+    for image in (a + b, a - b, c + d, c - d):
+        u, v, w, ox, oy, oz = [image[f] for f in range(6)]
+        products.append(jnp.stack([v * oz - w * oy, w * ox - u * oz, u * oy - v * ox], axis=0))
+    h1, h2, h3, h4 = [h.reshape(3 * block, width) for h in products]
+    sum1, sum2, dif1, dif2 = h1 + h2, h3 + h4, h1 - h2, h3 - h4
+    results = []
+    for g, h in enumerate((sum1 + sum2, sum1 - sum2, dif1 + dif2, dif1 - dif2)):
+        high, low = split(h)
+        results.append(dot3(high, low, tf_ref[0, g], tf_ref[1, g]))
+    for s in range(0, sources, 4):
+        at = (s // 4) * LANES
+        pieces = block_transpose([r[:, at : at + LANES] for r in results])
+        for k in range(4):
+            out_ref[s + k] = pieces[k].reshape(3, block, LANES)
+
+
+def span_forward_kernel(x_ref, t_ref, out_ref):
+    sources, fields, both, _ = x_ref.shape
+    step = both // 2
+    rows, half = out_ref.shape[0], out_ref.shape[3]
+    for parity in range(2):
+        columns = []
+        for f in range(fields):
+            first, second = x_ref[:, f, :step], x_ref[:, f, step:]
+            h = first + second if parity == 0 else first - second
+            h = h.reshape(sources * step, LANES)
+            columns.append(jnp.concatenate([h, -times_i(h)], axis=0))
+        high, low = split(jnp.concatenate(columns, axis=1))
+        result = dot3(t_ref[0, parity], t_ref[1, parity], high, low)
+        for row in range(rows):
+            for f in range(fields):
+                out_ref[row, f, parity] = result[
+                    row * half : (row + 1) * half, f * LANES : (f + 1) * LANES
+                ]
+
+
+def combine_kernel(*refs, chunks, rows, count):
+    h_refs = refs[:chunks]
+    kx_ref, kz_ref, w_ref, vort_ref, lapv_ref, terms, *sums = refs[chunks:]
+    kx = kx_ref[...]
+    padded = terms.shape[0] // 16
+    if padded > 3 * count:
+        terms[3 * count * 16 :, :] = jnp.zeros(((padded - 3 * count) * 16, LANES), F32)
+    for parity in range(2):
+        kz = kz_ref[parity]
+        square = kx * kx + kz * kz
+        damp_g = 1.0 / jnp.sqrt(1.0 + square)
+        damp_v = 1.0 / (1.0 + square)
+        for chunk in range(chunks):
+            for row in range(rows):
+                p = chunk * rows + row
+                hx, hy, hz = [h_refs[chunk][row, f, parity] for f in range(3)]
+                members = (
+                    times_i(kz * hx - kx * hz) * damp_g,
+                    -times_i(kx * hx + kz * hz) * damp_v,
+                    -square * hy * damp_v,
+                )
+                for t, member in enumerate(members):
+                    at = (t * count + p) * 16 + parity * 8
+                    terms[at : at + 8, :] = member
+    for parity in range(2):
+        for half in range(8):
+            high, low = split(terms[pl.ds(parity * 8 + half, padded, stride=16), :])
+            stacked = jnp.concatenate([high, low, high], axis=0)
+            result = lax.dot_general(
+                stacked, w_ref[...], (((0,), (0,)), ((), ())), preferred_element_type=F32
+            )
+            for part in range(2):
+                for odd in range(2):
+                    start = part * 1024 + odd * 16 + 2 * half + parity
+                    at = part * 64 + odd * 32
+                    for j in range(4):
+                        sums[j][pl.ds(start, 32, stride=32), :] = result[
+                            at : at + 32, j * LANES : (j + 1) * LANES
+                        ]
+    shape = vort_ref.shape[:3] + (LANES,)
+    for j in range(2):
+        lanes = pl.ds(j * LANES, LANES)
+        vort_ref[:, :, :, lanes] = sums[j][...].reshape(shape)
+        lapv_ref[:, :, :, lanes] = sums[2 + j][...].reshape(shape)
+
+
+def exchange_kernel(*refs, jobs, sizes):
+    count = len(jobs)
+    sources, dests = refs[:count], refs[count : 2 * count]
+    send_sem, recv_sem, local_sem = refs[2 * count :]
+    position = {axis: lax.axis_index(axis) for axis in ("row", "col")}
+    axes = sorted({axis for axis, _ in jobs})
+    barrier = pltpu.get_barrier_semaphore()
+
+    def target(axis, offset):
+        return lax.rem(position[axis] + offset, sizes[axis])
+
+    def device(axis, index):
+        return (index, position["col"]) if axis == "row" else (position["row"], index)
+
+    total = 0
+    for axis in axes:
+        for offset in range(1, sizes[axis]):
+            total += 1
+            pl.semaphore_signal(
+                barrier,
+                inc=1,
+                device_id=device(axis, target(axis, offset)),
+                device_id_type=MESH,
+            )
+    pl.semaphore_wait(barrier, total)
+
+    def block(ref, axis, chunk, index):
+        return ref.at[index] if chunk is None else ref.at[:, chunk * sizes[axis] + index]
+
+    copies = []
+    slot = 0
+    for job, (axis, chunk) in enumerate(jobs):
+        me = position[axis]
+        for offset in range(1, sizes[axis]):
+            peer = target(axis, offset)
+            copy = pltpu.make_async_remote_copy(
+                src_ref=block(sources[job], axis, chunk, peer),
+                dst_ref=dests[job].at[me],
+                send_sem=send_sem.at[slot],
+                recv_sem=recv_sem.at[slot],
+                device_id=device(axis, peer),
+                device_id_type=MESH,
+            )
+            copy.start()
+            copies.append(copy)
+            slot += 1
+    for job, (axis, chunk) in enumerate(jobs):
+        me = position[axis]
+        own = pltpu.make_async_copy(
+            block(sources[job], axis, chunk, me), dests[job].at[me], local_sem.at[job]
+        )
+        own.start()
+        copies.append(own)
+    for copy in copies:
+        copy.wait()
+
+
+def exchange(jobs, arrays, sizes, collective_id):
+    shapes = []
+    for (axis, chunk), array in zip(jobs, arrays):
+        shape = array.shape
+        if chunk is not None:
+            shape = (sizes[axis], shape[0]) + shape[2:]
+        shapes.append(jax.ShapeDtypeStruct(shape, array.dtype))
+    slots = sum(sizes[axis] - 1 for axis, _ in jobs)
+    anywhere = pl.BlockSpec(memory_space=pl.ANY)
+    return pl.pallas_call(
+        functools.partial(exchange_kernel, jobs=tuple(jobs), sizes=sizes),
+        out_shape=shapes,
+        in_specs=[anywhere] * len(jobs),
+        out_specs=[anywhere] * len(jobs),
+        scratch_shapes=[
+            pltpu.SemaphoreType.DMA((slots,)),
+            pltpu.SemaphoreType.DMA((slots,)),
+            pltpu.SemaphoreType.DMA((len(jobs),)),
+        ],
+        compiler_params=pltpu.CompilerParams(collective_id=collective_id, has_side_effects=True),
+        name="exchange_%d" % collective_id,
+    )(*arrays)
+
+
+def rounded_halves(w):
+    high = lax.reduce_precision(w, 8, 7)
+    return high.astype(BF16), (w - high).astype(BF16)
+
+
+def pad_rows(w, rows):
+    return jnp.pad(w, ((0, rows - w.shape[0]), (0, 0)))
+
+
+def params(**extra):
+    return pltpu.CompilerParams(vmem_limit_bytes=VMEM_LIMIT, **extra)
+
+
+def whole(shape):
+    return pl.BlockSpec(shape, lambda *_: (0,) * len(shape))
+
+
+def per_device_fast(v_coef, vort_coef, plane_ops, inverse_ops, sizes):
+    rows, cols = sizes["row"], sizes["col"]
+    _, stream_local, span_local, coefs = v_coef.shape
+    count = plane_ops.shape[1]
+    chunks = count // rows
+    half = span_local // 2
+    modes = rows * half
+    stream_total, span_total = stream_local * cols, span_local * rows
+    points = 3 * span_total // 2
+    step = points // (2 * cols)
+    stream_points = 3 * stream_total
+
+    lane = jnp.arange(LANES, dtype=jnp.int32)
+    mode = 2 * (lane % 32) + (lane // 32) % 2 + stream_local * lax.axis_index("col")
+    kx = (STREAM_STEP * mode.astype(F32))[None, :]
+    signed = signed_order(rows, span_local, span_total)
+    kz_all = np.broadcast_to(
+        (np.float32(SPAN_STEP) * signed.astype(np.float32))[..., None], signed.shape + (LANES,)
+    )
+    n_here = (
+        span_local * lax.axis_index("row")
+        + jnp.arange(2, dtype=jnp.int32)[:, None]
+        + 2 * jnp.arange(half, dtype=jnp.int32)[None, :]
+    )
+    signed_here = jnp.where(n_here < span_total // 2, n_here, n_here - span_total)
+    kz_here = jnp.broadcast_to(
+        (SPAN_STEP * signed_here.astype(F32))[..., None], (2, half, LANES)
+    )
+    span_in, span_out = span_fast_tables(rows, span_local, span_total)
+    stream_in, stream_out = stream_fast_tables(stream_total)
+
+    weights = []
+    for ops, rows_used in ((plane_ops, 3), (plane_ops[:2], 2)):
+        flat = ops.reshape(rows_used * count, coefs)
+        padded = -(-rows_used * count // 16) * 16
+        weights.append(jnp.concatenate([pad_rows(w, padded) for w in rounded_halves(flat)], axis=0))
+
+    coef_spec = [
+        pl.BlockSpec((2, stream_local, 16, LANES), lambda i: (0, 0, i, 0)),
+        pl.BlockSpec((2, stream_local, 16, LANES), lambda i: (0, 0, i, 1)),
+    ]
+    values = pl.pallas_call(
+        functools.partial(plane_kernel, count=count),
+        grid=(span_local // 16,),
+        out_shape=jax.ShapeDtypeStruct((5 * count, 2, half, LANES), F32),
+        in_specs=coef_spec + coef_spec + [whole(w.shape) for w in weights],
+        out_specs=pl.BlockSpec((5 * count, 2, 8, LANES), lambda i: (0, 0, i, 0)),
+        compiler_params=params(),
+        name="plane_values",
+    )(v_coef, v_coef, vort_coef, vort_coef, *weights)
+    values = values.reshape(5, count, 2, half, LANES)
+
+    def span_inverse(received):
+        return pl.pallas_call(
+            functools.partial(span_inverse_kernel, rows=rows, half=half),
+            grid=(3,),
+            out_shape=jax.ShapeDtypeStruct((cols, 6, 2 * step, LANES), F32),
+            in_specs=[
+                whole((rows, 5, 2, half, LANES)),
+                whole((1, LANES)),
+                whole(kz_all.shape),
+                whole(span_in.shape),
+            ],
+            out_specs=pl.BlockSpec((cols, 2, 2 * step, LANES), lambda i: (0, i, 0, 0)),
+            scratch_shapes=[pltpu.VMEM((3, 2, 2 * modes, 2 * LANES), BF16)] * 2,
+            compiler_params=params(),
+            name="span_inverse",
+        )(received, kx, jnp.asarray(kz_all), jnp.asarray(span_in))
+
+    def stream_products(arrived):
+        block = 48
+        return pl.pallas_call(
+            stream_kernel,
+            grid=(2 * step // block,),
+            out_shape=jax.ShapeDtypeStruct((cols, 3, 2 * step, LANES), F32),
+            in_specs=[
+                pl.BlockSpec((cols, 6, block, LANES), lambda i: (0, 0, i, 0)),
+                whole(stream_in.shape),
+                whole(stream_out.shape),
+            ],
+            out_specs=pl.BlockSpec((cols, 3, block, LANES), lambda i: (0, 0, i, 0)),
+            compiler_params=params(),
+            name="stream_products",
+        )(arrived, jnp.asarray(stream_in), jnp.asarray(stream_out))
+
+    def span_forward(returned):
+        return pl.pallas_call(
+            span_forward_kernel,
+            out_shape=jax.ShapeDtypeStruct((rows, 3, 2, half, LANES), F32),
+            compiler_params=params(),
+            name="span_forward",
+        )(returned, jnp.asarray(span_out))
+
+    state = [values] * chunks
+    after = [span_inverse, stream_products, span_forward, lambda home: home]
+    axes = ["row", "col", "col", "row"]
+    for turn in range(chunks + 3):
+        active = [c for c in range(chunks) if 0 <= turn - c < 4]
+        jobs = [(axes[turn - c], c if turn == c else None) for c in active]
+        results = exchange(jobs, [state[c] for c in active], sizes, turn)
+        for c, result in zip(active, results):
+            state[c] = after[turn - c](result)
+
+    inv0, inv1 = inverse_ops[0].T, inverse_ops[1].T
+    none = jnp.zeros_like(inv0)
+    table = jnp.concatenate(
+        [
+            jnp.concatenate([inv0, none], axis=1),
+            jnp.concatenate([none, inv1], axis=1),
+            jnp.concatenate([none, inv0], axis=1),
+        ],
+        axis=0,
+    )
+    padded = -(-3 * count // 16) * 16
+    high, low = [pad_rows(w, padded) for w in rounded_halves(table)]
+    table = jnp.concatenate([high, high, low], axis=0)
+    out_block = pl.BlockSpec((2, stream_local, 16, coefs), lambda i: (0, 0, i, 0))
+    return pl.pallas_call(
+        functools.partial(combine_kernel, chunks=chunks, rows=rows, count=count),
+        grid=(span_local // 16,),
+        out_shape=[jax.ShapeDtypeStruct(v_coef.shape, F32)] * 2,
+        in_specs=[pl.BlockSpec((rows, 3, 2, 8, LANES), lambda i: (0, 0, 0, i, 0))] * chunks
+        + [
+            whole((1, LANES)),
+            pl.BlockSpec((2, 8, LANES), lambda i: (0, i, 0)),
+            whole(table.shape),
+        ],
+        out_specs=[out_block] * 2,
+        scratch_shapes=[pltpu.VMEM((padded * 16, LANES), F32)]
+        + [pltpu.VMEM((2 * stream_local * 16, LANES), F32)] * 4,
+        compiler_params=params(),
+        name="combinations",
+    )(*state, kx, kz_here, table)
 
 
 def signed_modes(first, count, total):
@@ -19,37 +515,28 @@
 
 def span_tables(total):
     points = 3 * total // 2
-    signed = signed_modes(0, total, total)
-    grid = jnp.arange(points, dtype=jnp.int32)
-    phase = jnp.mod(signed[:, None] * grid[None, :], points).astype(jnp.float32)
-    angle = phase * (2.0 * math.pi / points)
-    cosine = jnp.cos(angle)
-    sine = jnp.sin(angle)
-    inverse = jnp.stack(
-        [jnp.stack([cosine, sine], axis=1), jnp.stack([-sine, cosine], axis=1)], axis=0
-    )
-    factor = FORWARD_SCALE / points
-    forward = (
-        jnp.stack(
-            [jnp.stack([cosine.T, -sine.T], axis=1), jnp.stack([sine.T, cosine.T], axis=1)], axis=0
-        )
-        * factor
-    )
-    return (inverse, forward)
+    n = np.arange(total)
+    signed = np.where(n < total // 2, n, n - total)
+    angle = np.mod(signed[:, None] * np.arange(points)[None, :], points) * (2.0 * math.pi / points)
+    cosine, sine = np.cos(angle), np.sin(angle)
+    inverse = np.stack(
+        [np.stack([cosine, sine], axis=1), np.stack([-sine, cosine], axis=1)], axis=0
+    )
+    forward = np.stack(
+        [np.stack([cosine.T, -sine.T], axis=1), np.stack([sine.T, cosine.T], axis=1)], axis=0
+    ) * (FORWARD_SCALE / points)
+    return jnp.asarray(inverse, F32), jnp.asarray(forward, F32)
 
 
 def stream_tables(total):
     points = 3 * total
-    modes = jnp.arange(total, dtype=jnp.int32)
-    grid = jnp.arange(points, dtype=jnp.int32)
-    phase = jnp.mod(modes[:, None] * grid[None, :], points).astype(jnp.float32)
-    angle = phase * (2.0 * math.pi / points)
-    cosine = jnp.cos(angle)
-    sine = jnp.sin(angle)
-    weights = jnp.where(modes == 0, 1.0, 2.0).astype(jnp.float32)[:, None]
-    inverse = jnp.stack([weights * cosine, -weights * sine], axis=0) * INVERSE_SCALE
-    forward = jnp.stack([cosine.T, -sine.T], axis=1) * (1.0 / points)
-    return (inverse, forward)
+    modes = np.arange(total)
+    angle = np.mod(modes[:, None] * np.arange(points)[None, :], points) * (2.0 * math.pi / points)
+    cosine, sine = np.cos(angle), np.sin(angle)
+    weights = np.where(modes == 0, 1.0, 2.0)[:, None]
+    inverse = np.stack([weights * cosine, -weights * sine], axis=0) * INVERSE_SCALE
+    forward = np.stack([cosine.T, -sine.T], axis=1) / points
+    return jnp.asarray(inverse, F32), jnp.asarray(forward, F32)
 
 
 def rotate(pair, factor):
@@ -153,6 +640,17 @@
 def solution(mesh):
     in_specs = (P(None, "col", "row", None), P(None, "col", "row", None), P(), P())
     out_specs = (P(None, "col", "row", None), P(None, "col", "row", None))
-    return jax.shard_map(
-        per_device, mesh=mesh, in_specs=in_specs, out_specs=out_specs, check_vma=False
-    )
+    sizes = {"row": mesh.shape["row"], "col": mesh.shape["col"]}
+
+    def choose(v_coef, vort_coef, plane_ops, inverse_ops):
+        args = (v_coef, vort_coef, plane_ops, inverse_ops)
+        fits = (
+            2 * v_coef.shape[1] == LANES
+            and v_coef.shape[2] % 32 == 0
+            and v_coef.shape[3] == 2 * LANES
+            and plane_ops.shape[1] % sizes["row"] == 0
+            and sizes["col"] == 8
+        )
+        return per_device_fast(*args, sizes) if fits else per_device(*args)
+
+    return jax.shard_map(choose, mesh=mesh, in_specs=in_specs, out_specs=out_specs, check_vma=False)

time: 1280 us -> 467 us (0.36); the launches traced: 1260 us -> 466 us
  Pallas kernels: 0 us -> 429 us
  waiting for transfers between devices: 429 us -> 0 us
  matrix products: 305 us -> 0 us
  local copies, waits for them, and re-layouts: 285 us -> 35.5 us
  other arithmetic: 217 us -> 0.81 us
  starting transfers between devices: 24.3 us -> 0 us
    all_to_all x4 -> x0, waiting for transfers between devices: 429 us -> none  [the longest x1 182 us: per_device(): lax.all_to_all(fields, 'row', split_axis=1, concat_axis=4, tiled=True)]
    pallas_call x0 -> x17, Pallas kernels: none -> 429 us  [the longest x6 272 us: exchange(): pl.pallas_call(functools.partial(exchange_kernel, jobs=tuple(jobs), sizes...]
    dot_general x9 -> x0, matrix products: 305 us -> none  [the longest x3 77.8 us: contract(): jnp.einsum('jp,pxck->cxkj', matrix, join_pair(term), precision=PRECISE)]
    all_to_all x2 -> x0, other arithmetic: 134 us -> none  [the longest x1 102 us: per_device(): lax.all_to_all(span_phys, 'col', split_axis=4, concat_axis=3, tiled=True)]
    all_to_all x8 -> x0, local copies, waits for them, and re-layouts: 99.9 us -> none  [the longest x3 36.6 us: per_device(): lax.all_to_all(span_phys, 'col', split_axis=4, concat_axis=3, tiled=True)]
    unnamed x40 -> x74, local copies, waits for them, and re-layouts: 112 us -> 32.2 us
    transpose x2 -> x1, local copies, waits for them, and re-layouts: 40.9 us -> 0.01 us  [per_device_fast(): inv0, inv1 = (inverse_ops[0].T, inverse_ops[1].T)]
    neg x6 -> x0, other arithmetic: 28.9 us -> none  [the longest x1 14.4 us: span_tables(): -sine.T]
  transfers between devices with their start and end apart: 4 -> 0, of which waited for: 4 -> 0; matrix products, arithmetic and copies ran while one was open for 6% -> 0% of each run, Pallas kernels for 0% -> 0%
where the time goes in v1:
time: 467 us; the launch traced here: 466 us
  Pallas kernels  429 us (92%)
  local copies, waits for them, and re-layouts  35.5 us (8%)
    pallas_call x6, Pallas kernels, exchange(): pl.pallas_call(functools.partial(exchange_kernel, jobs=tuple(jobs), sizes...  272 us
    pallas_call x1, Pallas kernels, per_device_fast(): pl.pallas_call(functools.partial(combine_kernel, chunks=chunks, rows=rows...  64.4 us
    pallas_call x1, Pallas kernels, per_device_fast(): pl.pallas_call(functools.partial(plane_kernel, count=count), grid=(span_l...  40.6 us
    unnamed x74, local copies, waits for them, and re-layouts  32.2 us
    pallas_call x3, Pallas kernels, stream_products(): pl.pallas_call(stream_kernel, grid=(2 * step // block,), out_shape=jax.Sh...  23.1 us
    pallas_call x3, Pallas kernels, span_inverse(): pl.pallas_call(functools.partial(span_inverse_kernel, rows=rows, half=hal...  18.8 us

profile of v1, /device:TPU:8, one launch (start us, length us, event | category | flops | bytes accessed | tf_op | source)
XLA Modules:
  0.0 466.0 jit_solution(14622593972371325044)
XLA Ops:
  0.7 0.1 fusion.13
  0.8 0.8 fusion.20
  1.6 0.8 slice.9
  2.4 0.8 reshape.152
  3.3 0.7 fusion.1.refs_5_
  3.9 0.7 broadcast_in_dim.2.refs_4_
  4.7 40.6 %plane_values.1 = f32[60,2,96,128]{3,2,1,0:T(8,128)S(1)} custom-call(f32[2,64,192,256]{3,2,1,0:T(8,128)} %v1.1, f32[2,64,192,256]{3,2,1,0:T(8,128)} %v1.1, f32[2,64,192,256]{3,2,1,0:T(8,128)} %g1.1, f32[2,64,192,256]{3,2,1,0:T(8,128)} %g1.1, bf16[96,256]{1,0:T(8,128)(2,1)S(1)} %fusion.8.wv_ref, bf16[64,256]{1,0:T(8,128)(2,1)S(1)} %fusion.10.wg_ref), custom_call_target="tpu_custom_call" | custom-call | tf_op jit(solution)/shard_map/plane_values/pallas_call | solution.py:417
  45.3 0.0 copy-start
  45.3 2.6 copy-done
  47.9 46.0 %exchange_0.1.r_ref = f32[4,5,2,96,128]{4,3,2,1,0:T(8,128)} custom-call(f32[5,12,2,96,128]{4,3,2,1,0:T(8,128)} %bitcast.9), custom_call_target="tpu_custom_call" | custom-call | tf_op jit(solution)/shard_map/exchange_0/pallas_call | solution.py:344
  93.9 0.0 copy-done.36
  93.9 0.2 jit_solution_.3.kz_ref
  94.0 0.0 copy-done.2
  94.0 0.0 copy-start.13
  94.1 1.5 copy-done.13
  95.6 6.2 %span_inverse.3.refs_0_ = f32[8,6,144,128]{3,2,1,0:T(8,128)S(1)} custom-call(f32[4,5,2,96,128]{4,3,2,1,0:T(8,128)S(1)} %copy-done.13, f32[1,128]{1,0:T(1,128)S(1)} %fusion.18.kx_ref.refs_3_, f32[4,2,96,128]{3,2,1,0:T(8,128)S(1)} %jit_solution_.3.kz_ref, bf16[2,2,576,768]{3,2,1,0:T(8,128)(2,1)S(1)} %copy-done.2), custom_call_target="tpu_custom_call" | custom-call | tf_op jit(solution)/shard_map/span_inverse/pallas_call | solution.py:429
  101.8 0.0 copy-start.12
  101.8 1.8 copy-done.12
  103.6 0.8 copy-done.17
  104.4 45.7 %exchange_1.1 = (f32[8,6,144,128]{3,2,1,0:T(8,128)}, f32[4,5,2,96,128]{4,3,2,1,0:T(8,128)}) custom-call(f32[8,6,144,128]{3,2,1,0:T(8,128)} %copy-done.12, f32[5,12,2,96,128]{4,3,2,1,0:T(8,128)} %bitcast.10), custom_call_target="tpu_custom_call" | custom-call | tf_op jit(solution)/shard_map/exchange_1/pallas_call | solution.py:344
  150.1 0.0 copy-start.4
  150.1 1.4 copy-done.4
  151.5 1.4 copy-done.7
  152.9 2.0 copy-done.26
  154.9 7.6 %stream_products.3.refs_0_ = f32[8,3,144,128]{3,2,1,0:T(8,128)S(1)} custom-call(f32[8,6,144,128]{3,2,1,0:T(8,128)S(1)} %copy-done.26, bf16[2,4,256,384]{3,2,1,0:T(8,128)(2,1)S(1)} %copy-done.7, bf16[2,4,384,256]{3,2,1,0:T(8,128)(2,1)S(1)} %copy-done.4), custom_call_target="tpu_custom_call" | custom-call | tf_op jit(solution)/shard_map/stream_products/pallas_call | solution.py:447
  162.5 0.0 copy-start.16
  162.5 1.2 copy-done.16
  163.7 0.0 copy-done.18
  163.7 0.0 copy-done.28
  163.7 6.4 %span_inverse.4.refs_1_ = f32[8,6,144,128]{3,2,1,0:T(8,128)S(1)} custom-call(f32[4,5,2,96,128]{4,3,2,1,0:T(8,128)S(1)} %copy-done.28, f32[1,128]{1,0:T(1,128)S(1)} %fusion.18.kx_ref.refs_3_, f32[4,2,96,128]{3,2,1,0:T(8,128)S(1)} %copy-done.18, bf16[2,2,576,768]{3,2,1,0:T(8,128)(2,1)S(1)} %copy-done.2), custom_call_target="tpu_custom_call" | custom-call | tf_op jit(solution)/shard_map/span_inverse/pallas_call | solution.py:429
  170.1 0.0 copy-start.11
  170.1 1.8 copy-done.11
  171.9 60.7 %exchange_2.1 = (f32[8,3,144,128]{3,2,1,0:T(8,128)}, f32[8,6,144,128]{3,2,1,0:T(8,128)}, f32[4,5,2,96,128]{4,3,2,1,0:T(8,128)}) custom-call(f32[8,3,144,128]{3,2,1,0:T(8,128)} %copy-done.16, f32[8,6,144,128]{3,2,1,0:T(8,128)} %copy-done.11, f32[5,12,2,96,128]{4,3,2,1,0:T(8,128)} %bitcast.11), custom_call_target="tpu_custom_call" | custom-call | tf_op jit(solution)/shard_map/exchange_2/pallas_call | solution.py:344
  232.6 0.0 copy-done.1
  232.6 1.5 copy-done.29
  234.1 3.1 span_forward.3.refs_0_
  237.2 2.0 copy-done.25
  239.2 7.8 %stream_products.4.refs_1_ = f32[8,3,144,128]{3,2,1,0:T(8,128)S(1)} custom-call(f32[8,6,144,128]{3,2,1,0:T(8,128)S(1)} %copy-done.25, bf16[2,4,256,384]{3,2,1,0:T(8,128)(2,1)S(1)} %copy-done.8, bf16[2,4,384,256]{3,2,1,0:T(8,128)(2,1)S(1)} %copy-done.5), custom_call_target="tpu_custom_call" | custom-call | tf_op jit(solution)/shard_map/stream_products/pallas_call | solution.py:447
  247.1 0.0 copy-start.14
  247.1 1.2 copy-done.14
  248.3 6.2 %span_inverse.5.refs_2_ = f32[8,6,144,128]{3,2,1,0:T(8,128)S(1)} custom-call(f32[4,5,2,96,128]{4,3,2,1,0:T(8,128)S(1)} %copy-done.27, f32[1,128]{1,0:T(1,128)S(1)} %fusion.18.kx_ref.refs_3_, f32[4,2,96,128]{3,2,1,0:T(8,128)S(1)} %copy-done.19, bf16[2,2,576,768]{3,2,1,0:T(8,128)(2,1)S(1)} %copy-done.3), custom_call_target="tpu_custom_call" | custom-call | tf_op jit(solution)/shard_map/span_inverse/pallas_call | solution.py:429
  254.5 0.0 copy-start.10
  254.5 1.8 copy-done.10
  256.3 60.9 %exchange_3.1 = (f32[4,3,2,96,128]{4,3,2,1,0:T(8,128)}, f32[8,3,144,128]{3,2,1,0:T(8,128)}, f32[8,6,144,128]{3,2,1,0:T(8,128)}) custom-call(f32[4,3,2,96,128]{4,3,2,1,0:T(8,128)} %copy-done.20, f32[8,3,144,128]{3,2,1,0:T(8,128)} %copy-done.14, f32[8,6,144,128]{3,2,1,0:T(8,128)} %copy-done.10), custom_call_target="tpu_custom_call" | custom-call | tf_op jit(solution)/shard_map/exchange_3/pallas_call | solution.py:344
  317.3 1.5 copy-done.30
  318.7 3.1 span_forward.4.refs_0_
  321.8 0.0 copy-start.22
  321.9 1.0 copy-done.22
  322.9 0.0 copy-done.9
  322.9 2.0 copy-done.24
  324.9 7.6 %stream_products.5.refs_1_ = f32[8,3,144,128]{3,2,1,0:T(8,128)S(1)} custom-call(f32[8,6,144,128]{3,2,1,0:T(8,128)S(1)} %copy-done.24, bf16[2,4,256,384]{3,2,1,0:T(8,128)(2,1)S(1)} %copy-done.9, bf16[2,4,384,256]{3,2,1,0:T(8,128)(2,1)S(1)} %copy-done.6), custom_call_target="tpu_custom_call" | custom-call | tf_op jit(solution)/shard_map/stream_products/pallas_call | solution.py:447
  332.5 0.0 copy-start.15
  332.5 1.2 copy-done.15
  333.7 30.8 %exchange_4.1 = (f32[4,3,2,96,128]{4,3,2,1,0:T(8,128)}, f32[8,3,144,128]{3,2,1,0:T(8,128)}) custom-call(f32[4,3,2,96,128]{4,3,2,1,0:T(8,128)} %copy-done.22, f32[8,3,144,128]{3,2,1,0:T(8,128)} %copy-done.15), custom_call_target="tpu_custom_call" | custom-call | tf_op jit(solution)/shard_map/exchange_4/pallas_call | solution.py:344
  364.5 0.0 copy-start.31
  364.5 1.5 copy-done.31
  366.0 3.1 span_forward.5.refs_0_
  369.1 0.0 copy-start.21
  369.1 1.0 copy-done.21
  370.1 28.4 %exchange_5.1.refs_2_ = f32[4,3,2,96,128]{4,3,2,1,0:T(8,128)} custom-call(f32[4,3,2,96,128]{4,3,2,1,0:T(8,128)} %copy-done.21), custom_call_target="tpu_custom_call" | custom-call | tf_op jit(solution)/shard_map/exchange_5/pallas_call | solution.py:344
  398.5 1.3 copy-done.23
  399.8 0.9 copy-done.34
  400.7 0.9 copy-done.35
  401.6 64.4 %combinations.1 = (f32[2,64,192,256]{3,2,1,0:T(8,128)}, f32[2,64,192,256]{3,2,1,0:T(8,128)}) custom-call(f32[4,3,2,96,128]{4,3,2,1,0:T(8,128)S(1)} %copy-done.32, f32[4,3,2,96,128]{4,3,2,1,0:T(8,128)S(1)} %copy-done.33, f32[4,3,2,96,128]{4,3,2,1,0:T(8,128)S(1)} %copy-done.23, f32[1,128]{1,0:T(1,128)S(1)} %fusion.18.kx_ref.refs_3_, ...), custom_call_target="tpu_custom_call" | custom-call | tf_op jit(solution)/shard_map/combinations/pallas_call | solution.py:493
  (45 shorter events, 0.2 us)
Async XLA Ops:
  45.3 2.6 copy-start
  47.9 46.0 %copy-start.36 = (f32[4,2,96]{2,1,0:T(2,128)S(1)}, f32[4,2,96]{2,1,0:T(2,128)}, u32[]{:S(2)}) copy-start(f32[4,2,96]{2,1,0:T(2,128)} %constant.79.clone) | copy-start | bytes 9220
  47.9 46.2 %copy-start.2 = (bf16[2,2,576,768]{3,2,1,0:T(8,128)(2,1)S(1)}, bf16[2,2,576,768]{3,2,1,0:T(8,128)(2,1)}, u32[]{:S(2)}) copy-start(bf16[2,2,576,768]{3,2,1,0:T(8,128)(2,1)} %constant.80.clone.t_ref) | copy-start | bytes 10616836
  94.0 1.5 copy-start.13
  101.8 1.8 copy-start.12
  103.6 0.8 copy-start.17
  150.1 1.4 copy-start.4
  151.5 1.4 copy-start.7
  152.9 2.0 copy-start.26
  154.9 8.8 %copy-start.18 = (f32[4,2,96,128]{3,2,1,0:T(8,128)S(1)}, f32[4,2,96,128]{3,2,1,0:T(8,128)}, u32[]{:S(2)}) copy-start(f32[4,2,96,128]{3,2,1,0:T(8,128)} %copy-done.17) | copy-start | bytes 1179652
  154.9 8.8 %copy-start.28 = (f32[4,5,2,96,128]{4,3,2,1,0:T(8,128)S(1)}, f32[4,5,2,96,128]{4,3,2,1,0:T(8,128)}, u32[]{:S(2)}) copy-start(f32[4,5,2,96,128]{4,3,2,1,0:T(8,128)} %get-tuple-element.13.r_ref) | copy-start | bytes 5898244
  162.5 1.2 copy-start.16
  170.1 1.8 copy-start.11
  171.9 60.7 %copy-start.1 = (bf16[2,2,384,1152]{3,2,1,0:T(8,128)(2,1)S(1)}, bf16[2,2,384,1152]{3,2,1,0:T(8,128)(2,1)}, u32[]{:S(2)}) copy-start(bf16[2,2,384,1152]{3,2,1,0:T(8,128)(2,1)} %constant.83.clone.t_ref) | copy-start | bytes 10616836
  232.6 1.5 copy-start.29
  234.1 3.1 copy-start.5
  234.1 3.1 copy-start.8
  237.2 2.0 copy-start.25
  239.2 7.8 %copy-start.20 = (f32[4,3,2,96,128]{4,3,2,1,0:T(8,128)}, f32[4,3,2,96,128]{4,3,2,1,0:T(8,128)S(1)}, u32[]{:S(2)}) copy-start(f32[4,3,2,96,128]{4,3,2,1,0:T(8,128)S(1)} %span_forward.3.refs_0_) | copy-start | bytes 3538948
  239.2 9.0 %copy-start.3 = (bf16[2,2,576,768]{3,2,1,0:T(8,128)(2,1)S(1)}, bf16[2,2,576,768]{3,2,1,0:T(8,128)(2,1)}, u32[]{:S(2)}) copy-start(bf16[2,2,576,768]{3,2,1,0:T(8,128)(2,1)} %constant.80.clone.t_ref) | copy-start | bytes 10616836
  239.2 9.0 %copy-start.19 = (f32[4,2,96,128]{3,2,1,0:T(8,128)S(1)}, f32[4,2,96,128]{3,2,1,0:T(8,128)}, u32[]{:S(2)}) copy-start(f32[4,2,96,128]{3,2,1,0:T(8,128)} %copy-done.17) | copy-start | bytes 1179652
  239.2 9.0 %copy-start.27 = (f32[4,5,2,96,128]{4,3,2,1,0:T(8,128)S(1)}, f32[4,5,2,96,128]{4,3,2,1,0:T(8,128)}, u32[]{:S(2)}) copy-start(f32[4,5,2,96,128]{4,3,2,1,0:T(8,128)} %get-tuple-element.16.r_ref) | copy-start | bytes 5898244
  247.1 1.2 copy-start.14
  254.5 1.8 copy-start.10
  317.3 1.5 copy-start.30
  318.7 4.1 copy-start.6
  318.7 4.1 copy-start.9
  321.8 1.0 copy-start.22
  322.9 2.0 copy-start.24
  332.5 1.2 copy-start.15
  364.5 1.5 copy-start.31
  369.1 1.0 copy-start.21
  370.1 28.4 %copy-start.32 = (f32[4,3,2,96,128]{4,3,2,1,0:T(8,128)S(1)}, f32[4,3,2,96,128]{4,3,2,1,0:T(8,128)}, u32[]{:S(2)}) copy-start(f32[4,3,2,96,128]{4,3,2,1,0:T(8,128)} %get-tuple-element.17.refs_0_) | copy-start | bytes 3538948
  370.1 28.4 %copy-start.33 = (f32[4,3,2,96,128]{4,3,2,1,0:T(8,128)S(1)}, f32[4,3,2,96,128]{4,3,2,1,0:T(8,128)}, u32[]{:S(2)}) copy-start(f32[4,3,2,96,128]{4,3,2,1,0:T(8,128)} %get-tuple-element.20.refs_1_) | copy-start | bytes 3538948
  398.5 1.3 copy-start.23
  399.8 0.9 copy-start.34
  400.7 0.9 copy-start.35

commit v2 on v1

--- a/solution.py
+++ b/solution.py
@@ -106,35 +106,26 @@
     return lax.dot_general(a, b, (((1,), (1,)), ((), ())), preferred_element_type=F32)
 
 
-def plane_kernel(v0, v1, g0, g1, wv_ref, wg_ref, out_ref, *, count):
-    flat = out_ref.reshape(out_ref.shape[0] * 16, LANES)
-    base = 0
-    for low_ref, high_ref, w_ref, ops in ((v0, v1, wv_ref, 3), (g0, g1, wg_ref, 2)):
-        refs = [ref.reshape(2 * 64 * 16, LANES) for ref in (low_ref, high_ref)]
-        pad = w_ref.shape[0] // 2
-        for parity in range(2):
-            for pair in range(4):
-                rows = []
-                for half in (2 * pair, 2 * pair + 1):
-                    for part in range(2):
-                        for odd in range(2):
-                            start = part * 1024 + odd * 16 + 2 * half + parity
-                            rows.append(
-                                jnp.concatenate(
-                                    [ref[pl.ds(start, 32, stride=32), :] for ref in refs], axis=1
-                                )
-                            )
-                high, low = split(jnp.concatenate(rows, axis=0))
-                first = contract_last(w_ref[...], high)
-                second = contract_last(w_ref[:pad], low)
-                sums = first[:pad] + (first[pad:] + second)
-                used = ops * count
-                for side in range(2):
-                    at = base * 16 + parity * 8 + 2 * pair + side
-                    flat[pl.ds(at, used, stride=16), :] = sums[
-                        :used, side * LANES : (side + 1) * LANES
-                    ]
-        base += ops * count
+def plane_kernel(v_ref, g_ref, first_ref, second_ref, out_ref, y_ref):
+    used = out_ref.shape[0]
+    flat = out_ref.reshape(used * 16, LANES)
+    for part in range(2):
+        for side in range(2):
+            at = pl.ds(side * 32, 32)
+            rows = [ref[part, at].reshape(512, 2 * LANES) for ref in (v_ref, g_ref)]
+            high, low = split(jnp.concatenate(rows, axis=1))
+            y = dot(high, first_ref[...])
+            y = y + pltpu.roll(y, LANES // 2, 1) + dot(low, second_ref[...])
+            y_ref[pl.ds((2 * part + side) * 512, 512), :] = y
+    for parity in range(2):
+        for half in range(8):
+            rows = []
+            for part in range(2):
+                for odd in range(2):
+                    start = part * 1024 + odd * 16 + 2 * half + parity
+                    rows.append(y_ref[pl.ds(start, 32, stride=32), :])
+            turned = jnp.concatenate(rows, axis=0).T
+            flat[pl.ds(parity * 8 + half, used, stride=16), :] = turned[:used]
 
 
 def span_inverse_kernel(r_ref, kx_ref, kz_ref, t_ref, out_ref, high_ref, low_ref, *, rows, half):
@@ -231,7 +222,7 @@
 
 def combine_kernel(*refs, chunks, rows, count):
     h_refs = refs[:chunks]
-    kx_ref, kz_ref, w_ref, vort_ref, lapv_ref, terms, *sums = refs[chunks:]
+    kx_ref, kz_ref, w_ref, vort_ref, lapv_ref, terms, left = refs[chunks:]
     kx = kx_ref[...]
     padded = terms.shape[0] // 16
     if padded > 3 * count:
@@ -255,24 +246,21 @@
                     terms[at : at + 8, :] = member
     for parity in range(2):
         for half in range(8):
-            high, low = split(terms[pl.ds(parity * 8 + half, padded, stride=16), :])
-            stacked = jnp.concatenate([high, low, high], axis=0)
-            result = lax.dot_general(
-                stacked, w_ref[...], (((0,), (0,)), ((), ())), preferred_element_type=F32
-            )
+            values = terms[pl.ds(parity * 8 + half, padded, stride=16), :]
+            high = values.astype(BF16).astype(F32)
+            rest = jnp.zeros((LANES - 3 * padded, LANES), F32)
+            turned = jnp.concatenate([high, values - high, high, rest], axis=0).T
             for part in range(2):
                 for odd in range(2):
                     start = part * 1024 + odd * 16 + 2 * half + parity
                     at = part * 64 + odd * 32
-                    for j in range(4):
-                        sums[j][pl.ds(start, 32, stride=32), :] = result[
-                            at : at + 32, j * LANES : (j + 1) * LANES
-                        ]
-    shape = vort_ref.shape[:3] + (LANES,)
-    for j in range(2):
-        lanes = pl.ds(j * LANES, LANES)
-        vort_ref[:, :, :, lanes] = sums[j][...].reshape(shape)
-        lapv_ref[:, :, :, lanes] = sums[2 + j][...].reshape(shape)
+                    left[pl.ds(start, 32, stride=32), :] = turned[at : at + 32]
+    for part in range(2):
+        for side in range(2):
+            rows = left[pl.ds((2 * part + side) * 512, 512), :].astype(BF16)
+            result = dot(rows, w_ref[...]).reshape(32, 16, 4 * LANES)
+            vort_ref[part, pl.ds(side * 32, 32)] = result[:, :, : 2 * LANES]
+            lapv_ref[part, pl.ds(side * 32, 32)] = result[:, :, 2 * LANES :]
 
 
 def exchange_kernel(*refs, jobs, sizes):
@@ -404,25 +392,29 @@
     span_in, span_out = span_fast_tables(rows, span_local, span_total)
     stream_in, stream_out = stream_fast_tables(stream_total)
 
-    weights = []
-    for ops, rows_used in ((plane_ops, 3), (plane_ops[:2], 2)):
-        flat = ops.reshape(rows_used * count, coefs)
-        padded = -(-rows_used * count // 16) * 16
-        weights.append(jnp.concatenate([pad_rows(w, padded) for w in rounded_halves(flat)], axis=0))
-
-    coef_spec = [
-        pl.BlockSpec((2, stream_local, 16, LANES), lambda i: (0, 0, i, 0)),
-        pl.BlockSpec((2, stream_local, 16, LANES), lambda i: (0, 0, i, 1)),
+    used = 5 * count
+    highs, lows = [], []
+    for ops, before, after in ((plane_ops, 0, 2), (plane_ops[:2], 3, 0)):
+        flat = ops.reshape(-1, coefs).T
+        for kept, w in zip((highs, lows), rounded_halves(flat)):
+            kept.append(jnp.pad(w, ((0, 0), (before * count, after * count + 64 - used))))
+    high, low = [jnp.concatenate(kept, axis=0) for kept in (highs, lows)]
+    weights = [
+        jnp.concatenate([high, low], axis=1),
+        jnp.concatenate([high, jnp.zeros_like(high)], axis=1),
     ]
+
+    coef_spec = pl.BlockSpec((2, stream_local, 16, coefs), lambda i: (0, 0, i, 0))
     values = pl.pallas_call(
-        functools.partial(plane_kernel, count=count),
+        plane_kernel,
         grid=(span_local // 16,),
         out_shape=jax.ShapeDtypeStruct((5 * count, 2, half, LANES), F32),
-        in_specs=coef_spec + coef_spec + [whole(w.shape) for w in weights],
+        in_specs=[coef_spec] * 2 + [whole(w.shape) for w in weights],
         out_specs=pl.BlockSpec((5 * count, 2, 8, LANES), lambda i: (0, 0, i, 0)),
+        scratch_shapes=[pltpu.VMEM((2 * stream_local * 16, LANES), F32)],
         compiler_params=params(),
         name="plane_values",
-    )(v_coef, v_coef, vort_coef, vort_coef, *weights)
+    )(v_coef, vort_coef, *weights)
     values = values.reshape(5, count, 2, half, LANES)
 
     def span_inverse(received):
@@ -486,9 +478,9 @@
         ],
         axis=0,
     )
-    padded = -(-3 * count // 16) * 16
+    padded = -(-3 * count // 8) * 8
     high, low = [pad_rows(w, padded) for w in rounded_halves(table)]
-    table = jnp.concatenate([high, high, low], axis=0)
+    table = pad_rows(jnp.concatenate([high, high, low], axis=0), LANES)
     out_block = pl.BlockSpec((2, stream_local, 16, coefs), lambda i: (0, 0, i, 0))
     return pl.pallas_call(
         functools.partial(combine_kernel, chunks=chunks, rows=rows, count=count),
@@ -502,7 +494,7 @@
         ],
         out_specs=[out_block] * 2,
         scratch_shapes=[pltpu.VMEM((padded * 16, LANES), F32)]
-        + [pltpu.VMEM((2 * stream_local * 16, LANES), F32)] * 4,
+        + [pltpu.VMEM((2 * stream_local * 16, LANES), F32)],
         compiler_params=params(),
         name="combinations",
     )(*state, kx, kz_here, table)
@@ -649,6 +641,7 @@
             and v_coef.shape[2] % 32 == 0
             and v_coef.shape[3] == 2 * LANES
             and plane_ops.shape[1] % sizes["row"] == 0
+            and plane_ops.shape[1] <= 12
             and sizes["col"] == 8
         )
         return per_device_fast(*args, sizes) if fits else per_device(*args)

time: 467 us -> 414 us (0.89)
  Pallas kernels: 429 us -> 375 us
    pallas_call x1, Pallas kernels: 64.4 us -> 23.5 us  [per_device_fast(): pl.pallas_call(functools.partial(combine_kernel, chunks=chunks, rows=rows...]
    pallas_call x1, Pallas kernels: 40.6 us -> 28 us  [per_device_fast(): pl.pallas_call(plane_kernel, grid=(span_local // 16,), out_shape=jax.Shap...]
where the time goes in v2:
time: 414 us; the launch traced here: 413 us
  Pallas kernels  375 us (91%)
  local copies, waits for them, and re-layouts  36.5 us (9%)
    pallas_call x6, Pallas kernels, exchange(): pl.pallas_call(functools.partial(exchange_kernel, jobs=tuple(jobs), sizes...  272 us
    unnamed x74, local copies, waits for them, and re-layouts  32.2 us
    pallas_call x1, Pallas kernels, per_device_fast(): pl.pallas_call(plane_kernel, grid=(span_local // 16,), out_shape=jax.Shap...  28 us
    pallas_call x1, Pallas kernels, per_device_fast(): pl.pallas_call(functools.partial(combine_kernel, chunks=chunks, rows=rows...  23.5 us
    pallas_call x3, Pallas kernels, stream_products(): pl.pallas_call(stream_kernel, grid=(2 * step // block,), out_shape=jax.Sh...  23.1 us
    pallas_call x3, Pallas kernels, span_inverse(): pl.pallas_call(functools.partial(span_inverse_kernel, rows=rows, half=hal...  18.8 us
    pallas_call x3, Pallas kernels, span_forward(): pl.pallas_call(span_forward_kernel, out_shape=jax.ShapeDtypeStruct((rows,...  9.29 us

profile of v2, /device:TPU:8, one launch (start us, length us, event | category | flops | bytes accessed | tf_op | source)
XLA Modules:
  0.0 413.0 jit_solution(5526101846828874197)
XLA Ops:
  0.7 0.1 fusion.18
  0.8 0.8 fusion.25
  1.6 0.8 slice.9
  2.4 0.8 reshape.152
  3.2 0.7 pad.35.refs_5_
  3.9 0.1 copy.15
  4.1 0.7 broadcast_in_dim.2.refs_4_
  4.8 0.1 copy.16
  4.9 0.1 pad.30
  5.0 0.1 fusion.13
  5.1 28.0 %plane_values.1 = f32[60,2,96,128]{3,2,1,0:T(8,128)S(1)} custom-call(f32[2,64,192,256]{3,2,1,0:T(8,128)} %v_ref.1, f32[2,64,192,256]{3,2,1,0:T(8,128)} %g_ref.1, bf16[512,128]{1,0:T(8,128)(2,1)S(1)} %get-tuple-element.23.first_ref, bf16[512,128]{1,0:T(8,128)(2,1)S(1)} %get-tuple-element.22.second_ref), custom_call_target="tpu_custom_call" | custom-call | tf_op jit(solution)/shard_map/plane_values/pallas_call | solution.py:408
  33.1 0.0 copy-start
  33.1 2.6 copy-done
  35.7 46.0 %exchange_0.1.r_ref = f32[4,5,2,96,128]{4,3,2,1,0:T(8,128)} custom-call(f32[5,12,2,96,128]{4,3,2,1,0:T(8,128)} %bitcast.15), custom_call_target="tpu_custom_call" | custom-call | tf_op jit(solution)/shard_map/exchange_0/pallas_call | solution.py:332
  81.7 0.2 jit_solution_.3.kz_ref
  81.9 1.5 copy-done.13
  83.5 6.2 %span_inverse.3.refs_0_ = f32[8,6,144,128]{3,2,1,0:T(8,128)S(1)} custom-call(f32[4,5,2,96,128]{4,3,2,1,0:T(8,128)S(1)} %copy-done.13, f32[1,128]{1,0:T(1,128)S(1)} %fusion.23.kx_ref.refs_3_, f32[4,2,96,128]{3,2,1,0:T(8,128)S(1)} %jit_solution_.3.kz_ref, bf16[2,2,576,768]{3,2,1,0:T(8,128)(2,1)S(1)} %copy-done.2), custom_call_target="tpu_custom_call" | custom-call | tf_op jit(solution)/shard_map/span_inverse/pallas_call | solution.py:421
  89.7 0.0 copy-start.12
  89.7 1.8 copy-done.12
  91.5 0.7 copy-done.17
  92.2 45.7 %exchange_1.1 = (f32[8,6,144,128]{3,2,1,0:T(8,128)}, f32[4,5,2,96,128]{4,3,2,1,0:T(8,128)}) custom-call(f32[8,6,144,128]{3,2,1,0:T(8,128)} %copy-done.12, f32[5,12,2,96,128]{4,3,2,1,0:T(8,128)} %bitcast.16), custom_call_target="tpu_custom_call" | custom-call | tf_op jit(solution)/shard_map/exchange_1/pallas_call | solution.py:332
  137.9 0.0 copy-start.4
  137.9 1.4 copy-done.4
  139.3 1.4 copy-done.7
  140.7 2.0 copy-done.26
  142.7 7.6 %stream_products.3.refs_0_ = f32[8,3,144,128]{3,2,1,0:T(8,128)S(1)} custom-call(f32[8,6,144,128]{3,2,1,0:T(8,128)S(1)} %copy-done.26, bf16[2,4,256,384]{3,2,1,0:T(8,128)(2,1)S(1)} %copy-done.7, bf16[2,4,384,256]{3,2,1,0:T(8,128)(2,1)S(1)} %copy-done.4), custom_call_target="tpu_custom_call" | custom-call | tf_op jit(solution)/shard_map/stream_products/pallas_call | solution.py:439
  150.4 1.2 copy-done.16
  151.6 0.0 copy-done.28
  151.6 6.4 %span_inverse.4.refs_1_ = f32[8,6,144,128]{3,2,1,0:T(8,128)S(1)} custom-call(f32[4,5,2,96,128]{4,3,2,1,0:T(8,128)S(1)} %copy-done.28, f32[1,128]{1,0:T(1,128)S(1)} %fusion.23.kx_ref.refs_3_, f32[4,2,96,128]{3,2,1,0:T(8,128)S(1)} %copy-done.18, bf16[2,2,576,768]{3,2,1,0:T(8,128)(2,1)S(1)} %copy-done.2), custom_call_target="tpu_custom_call" | custom-call | tf_op jit(solution)/shard_map/span_inverse/pallas_call | solution.py:421
  158.0 0.0 copy-start.11
  158.0 1.8 copy-done.11
  159.8 60.7 %exchange_2.1 = (f32[8,3,144,128]{3,2,1,0:T(8,128)}, f32[8,6,144,128]{3,2,1,0:T(8,128)}, f32[4,5,2,96,128]{4,3,2,1,0:T(8,128)}) custom-call(f32[8,3,144,128]{3,2,1,0:T(8,128)} %copy-done.16, f32[8,6,144,128]{3,2,1,0:T(8,128)} %copy-done.11, f32[5,12,2,96,128]{4,3,2,1,0:T(8,128)} %bitcast.17), custom_call_target="tpu_custom_call" | custom-call | tf_op jit(solution)/shard_map/exchange_2/pallas_call | solution.py:332
  220.5 1.5 copy-done.29
  222.0 3.1 span_forward.3.refs_0_
  225.1 2.0 copy-done.25
  227.1 7.8 %stream_products.4.refs_1_ = f32[8,3,144,128]{3,2,1,0:T(8,128)S(1)} custom-call(f32[8,6,144,128]{3,2,1,0:T(8,128)S(1)} %copy-done.25, bf16[2,4,256,384]{3,2,1,0:T(8,128)(2,1)S(1)} %copy-done.8, bf16[2,4,384,256]{3,2,1,0:T(8,128)(2,1)S(1)} %copy-done.5), custom_call_target="tpu_custom_call" | custom-call | tf_op jit(solution)/shard_map/stream_products/pallas_call | solution.py:439
  234.9 0.0 copy-start.14
  234.9 1.2 copy-done.14
  236.1 0.0 copy-done.19
  236.1 6.2 %span_inverse.5.refs_2_ = f32[8,6,144,128]{3,2,1,0:T(8,128)S(1)} custom-call(f32[4,5,2,96,128]{4,3,2,1,0:T(8,128)S(1)} %copy-done.27, f32[1,128]{1,0:T(1,128)S(1)} %fusion.23.kx_ref.refs_3_, f32[4,2,96,128]{3,2,1,0:T(8,128)S(1)} %copy-done.19, bf16[2,2,576,768]{3,2,1,0:T(8,128)(2,1)S(1)} %copy-done.3), custom_call_target="tpu_custom_call" | custom-call | tf_op jit(solution)/shard_map/span_inverse/pallas_call | solution.py:421
  242.4 0.0 copy-start.10
  242.4 1.8 copy-done.10
  244.2 60.9 %exchange_3.1 = (f32[4,3,2,96,128]{4,3,2,1,0:T(8,128)}, f32[8,3,144,128]{3,2,1,0:T(8,128)}, f32[8,6,144,128]{3,2,1,0:T(8,128)}) custom-call(f32[4,3,2,96,128]{4,3,2,1,0:T(8,128)} %copy-done.20, f32[8,3,144,128]{3,2,1,0:T(8,128)} %copy-done.14, f32[8,6,144,128]{3,2,1,0:T(8,128)} %copy-done.10), custom_call_target="tpu_custom_call" | custom-call | tf_op jit(solution)/shard_map/exchange_3/pallas_call | solution.py:332
  305.1 1.5 copy-done.30
  306.6 3.1 span_forward.4.refs_0_
  309.7 0.0 copy-start.22
  309.7 1.0 copy-done.22
  310.7 2.0 copy-done.24
  312.7 7.6 %stream_products.5.refs_1_ = f32[8,3,144,128]{3,2,1,0:T(8,128)S(1)} custom-call(f32[8,6,144,128]{3,2,1,0:T(8,128)S(1)} %copy-done.24, bf16[2,4,256,384]{3,2,1,0:T(8,128)(2,1)S(1)} %copy-done.9, bf16[2,4,384,256]{3,2,1,0:T(8,128)(2,1)S(1)} %copy-done.6), custom_call_target="tpu_custom_call" | custom-call | tf_op jit(solution)/shard_map/stream_products/pallas_call | solution.py:439
  320.4 0.0 copy-start.15
  320.4 1.2 copy-done.15
  321.6 30.7 %exchange_4.1 = (f32[4,3,2,96,128]{4,3,2,1,0:T(8,128)}, f32[8,3,144,128]{3,2,1,0:T(8,128)}) custom-call(f32[4,3,2,96,128]{4,3,2,1,0:T(8,128)} %copy-done.22, f32[8,3,144,128]{3,2,1,0:T(8,128)} %copy-done.15), custom_call_target="tpu_custom_call" | custom-call | tf_op jit(solution)/shard_map/exchange_4/pallas_call | solution.py:332
  352.3 1.5 copy-done.31
  353.8 3.1 span_forward.5.refs_0_
  356.9 0.0 copy-start.21
  356.9 1.0 copy-done.21
  357.9 28.4 %exchange_5.1.refs_2_ = f32[4,3,2,96,128]{4,3,2,1,0:T(8,128)} custom-call(f32[4,3,2,96,128]{4,3,2,1,0:T(8,128)} %copy-done.21), custom_call_target="tpu_custom_call" | custom-call | tf_op jit(solution)/shard_map/exchange_5/pallas_call | solution.py:332
  386.3 0.0 copy-done.32
  386.4 0.0 copy-done.33
  386.4 0.0 copy-start.23
  386.4 1.3 copy-done.23
  387.6 0.9 copy-done.34
  388.5 0.9 copy-done.35
  389.4 23.5 %combinations.1 = (f32[2,64,192,256]{3,2,1,0:T(8,128)}, f32[2,64,192,256]{3,2,1,0:T(8,128)}) custom-call(f32[4,3,2,96,128]{4,3,2,1,0:T(8,128)S(1)} %copy-done.32, f32[4,3,2,96,128]{4,3,2,1,0:T(8,128)S(1)} %copy-done.33, f32[4,3,2,96,128]{4,3,2,1,0:T(8,128)S(1)} %copy-done.23, f32[1,128]{1,0:T(1,128)S(1)} %fusion.23.kx_ref.refs_3_, ...), custom_call_target="tpu_custom_call" | custom-call | tf_op jit(solution)/shard_map/combinations/pallas_call | solution.py:485
  (49 shorter events, 0.2 us)
Async XLA Ops:
  33.1 2.6 copy-start
  35.7 46.0 %copy-start.36 = (f32[4,2,96]{2,1,0:T(2,128)S(1)}, f32[4,2,96]{2,1,0:T(2,128)}, u32[]{:S(2)}) copy-start(f32[4,2,96]{2,1,0:T(2,128)} %constant.80.clone) | copy-start | bytes 9220
  35.7 46.2 %copy-start.2 = (bf16[2,2,576,768]{3,2,1,0:T(8,128)(2,1)S(1)}, bf16[2,2,576,768]{3,2,1,0:T(8,128)(2,1)}, u32[]{:S(2)}) copy-start(bf16[2,2,576,768]{3,2,1,0:T(8,128)(2,1)} %constant.81.clone.t_ref) | copy-start | bytes 10616836
  81.9 1.5 copy-start.13
  89.7 1.8 copy-start.12
  91.5 0.8 copy-start.17
  137.9 1.4 copy-start.4
  139.3 1.4 copy-start.7
  140.7 2.0 copy-start.26
  142.7 8.9 %copy-start.18 = (f32[4,2,96,128]{3,2,1,0:T(8,128)S(1)}, f32[4,2,96,128]{3,2,1,0:T(8,128)}, u32[]{:S(2)}) copy-start(f32[4,2,96,128]{3,2,1,0:T(8,128)} %copy-done.17) | copy-start | bytes 1179652
  142.7 8.9 %copy-start.28 = (f32[4,5,2,96,128]{4,3,2,1,0:T(8,128)S(1)}, f32[4,5,2,96,128]{4,3,2,1,0:T(8,128)}, u32[]{:S(2)}) copy-start(f32[4,5,2,96,128]{4,3,2,1,0:T(8,128)} %get-tuple-element.13.r_ref) | copy-start | bytes 5898244
  150.4 1.2 copy-start.16
  158.0 1.8 copy-start.11
  159.8 60.7 %copy-start.1 = (bf16[2,2,384,1152]{3,2,1,0:T(8,128)(2,1)S(1)}, bf16[2,2,384,1152]{3,2,1,0:T(8,128)(2,1)}, u32[]{:S(2)}) copy-start(bf16[2,2,384,1152]{3,2,1,0:T(8,128)(2,1)} %constant.84.clone.t_ref) | copy-start | bytes 10616836
  220.5 1.5 copy-start.29
  222.0 3.1 copy-start.5
  222.0 3.1 copy-start.8
  225.1 2.0 copy-start.25
  227.1 7.8 %copy-start.20 = (f32[4,3,2,96,128]{4,3,2,1,0:T(8,128)}, f32[4,3,2,96,128]{4,3,2,1,0:T(8,128)S(1)}, u32[]{:S(2)}) copy-start(f32[4,3,2,96,128]{4,3,2,1,0:T(8,128)S(1)} %span_forward.3.refs_0_) | copy-start | bytes 3538948
  227.1 9.0 %copy-start.3 = (bf16[2,2,576,768]{3,2,1,0:T(8,128)(2,1)S(1)}, bf16[2,2,576,768]{3,2,1,0:T(8,128)(2,1)}, u32[]{:S(2)}) copy-start(bf16[2,2,576,768]{3,2,1,0:T(8,128)(2,1)} %constant.81.clone.t_ref) | copy-start | bytes 10616836
  227.1 9.0 %copy-start.19 = (f32[4,2,96,128]{3,2,1,0:T(8,128)S(1)}, f32[4,2,96,128]{3,2,1,0:T(8,128)}, u32[]{:S(2)}) copy-start(f32[4,2,96,128]{3,2,1,0:T(8,128)} %copy-done.17) | copy-start | bytes 1179652
  227.1 9.0 %copy-start.27 = (f32[4,5,2,96,128]{4,3,2,1,0:T(8,128)S(1)}, f32[4,5,2,96,128]{4,3,2,1,0:T(8,128)}, u32[]{:S(2)}) copy-start(f32[4,5,2,96,128]{4,3,2,1,0:T(8,128)} %get-tuple-element.16.r_ref) | copy-start | bytes 5898244
  234.9 1.2 copy-start.14
  242.4 1.8 copy-start.10
  305.1 1.5 copy-start.30
  306.6 4.1 %copy-start.6 = (bf16[2,4,384,256]{3,2,1,0:T(8,128)(2,1)S(1)}, bf16[2,4,384,256]{3,2,1,0:T(8,128)(2,1)}, u32[]{:S(2)}) copy-start(bf16[2,4,384,256]{3,2,1,0:T(8,128)(2,1)} %constant.83.clone.tf_ref) | copy-start | bytes 4718596
  306.6 4.1 %copy-start.9 = (bf16[2,4,256,384]{3,2,1,0:T(8,128)(2,1)S(1)}, bf16[2,4,256,384]{3,2,1,0:T(8,128)(2,1)}, u32[]{:S(2)}) copy-start(bf16[2,4,256,384]{3,2,1,0:T(8,128)(2,1)} %constant.82.clone.ti_ref) | copy-start | bytes 4718596
  309.7 1.0 copy-start.22
  310.7 2.0 copy-start.24
  320.4 1.2 copy-start.15
  352.3 1.5 copy-start.31
  356.9 1.0 copy-start.21
  357.9 28.4 %copy-start.32 = (f32[4,3,2,96,128]{4,3,2,1,0:T(8,128)S(1)}, f32[4,3,2,96,128]{4,3,2,1,0:T(8,128)}, u32[]{:S(2)}) copy-start(f32[4,3,2,96,128]{4,3,2,1,0:T(8,128)} %get-tuple-element.17.refs_0_) | copy-start | bytes 3538948
  357.9 28.4 %copy-start.33 = (f32[4,3,2,96,128]{4,3,2,1,0:T(8,128)S(1)}, f32[4,3,2,96,128]{4,3,2,1,0:T(8,128)}, u32[]{:S(2)}) copy-start(f32[4,3,2,96,128]{4,3,2,1,0:T(8,128)} %get-tuple-element.20.refs_1_) | copy-start | bytes 3538948
  386.4 1.3 copy-start.23
  387.6 0.9 copy-start.34
  388.5 0.9 copy-start.35

commit v3 on v2

--- a/solution.py
+++ b/solution.py
@@ -16,7 +16,7 @@
 INVERSE_SCALE = 1.0 / 32.0
 FORWARD_SCALE = 32.0
 LANES = 128
-VMEM_LIMIT = 44 * 1024 * 1024
+VMEM_LIMIT = 26 * 1024 * 1024
 MESH = pl.DeviceIdType.MESH
 F32 = jnp.float32
 BF16 = jnp.bfloat16
@@ -106,8 +106,34 @@
     return lax.dot_general(a, b, (((1,), (1,)), ((), ())), preferred_element_type=F32)
 
 
-def plane_kernel(v_ref, g_ref, first_ref, second_ref, out_ref, y_ref):
+def plane_kernel(
+    v_ref, g_ref, first_ref, second_ref, out_ref, held_ref,
+    y_ref, staged, send_sem, recv_sem, local_sem, *, rows_count, steps
+):
     used = out_ref.shape[0]
+    count = used // 5
+    step = pl.program_id(0)
+    me, col = lax.axis_index("row"), lax.axis_index("col")
+    peers = [lax.rem(me + offset, rows_count) for offset in range(1, rows_count)]
+
+    @pl.when(step == 0)
+    def _():
+        barrier = pltpu.get_barrier_semaphore()
+        for peer in peers:
+            pl.semaphore_signal(barrier, inc=1, device_id=(peer, col), device_id_type=MESH)
+        pl.semaphore_wait(barrier, rows_count - 1)
+
+    def sent(index, slot):
+        at = pl.ds(pl.multiple_of(index * 8, 8), 8)
+        return pltpu.make_async_remote_copy(
+            src_ref=staged.at[peers[slot], :, :, at],
+            dst_ref=held_ref.at[me, :, :, at],
+            send_sem=send_sem.at[index, slot],
+            recv_sem=recv_sem.at[index, slot],
+            device_id=(peers[slot], col),
+            device_id_type=MESH,
+        )
+
     flat = out_ref.reshape(used * 16, LANES)
     for part in range(2):
         for side in range(2):
@@ -126,6 +152,24 @@
                     rows.append(y_ref[pl.ds(start, 32, stride=32), :])
             turned = jnp.concatenate(rows, axis=0).T
             flat[pl.ds(parity * 8 + half, used, stride=16), :] = turned[:used]
+    here = pl.ds(pl.multiple_of(step * 8, 8), 8)
+    for row in range(rows_count):
+        for r in range(5):
+            staged[row, r, :, here] = out_ref[r * count + row]
+    for slot in range(rows_count - 1):
+        sent(step, slot).start()
+
+    @pl.when(step == steps - 1)
+    def _():
+        own = pltpu.make_async_copy(staged.at[me], held_ref.at[me], local_sem)
+        own.start()
+
+        @pl.loop(0, steps)
+        def _(index):
+            for slot in range(rows_count - 1):
+                sent(index, slot).wait()
+
+        own.wait()
 
 
 def span_inverse_kernel(r_ref, kx_ref, kz_ref, t_ref, out_ref, high_ref, low_ref, *, rows, half):
@@ -405,14 +449,27 @@
     ]
 
     coef_spec = pl.BlockSpec((2, stream_local, 16, coefs), lambda i: (0, 0, i, 0))
-    values = pl.pallas_call(
-        plane_kernel,
-        grid=(span_local // 16,),
-        out_shape=jax.ShapeDtypeStruct((5 * count, 2, half, LANES), F32),
+    steps = span_local // 16
+    values, held = pl.pallas_call(
+        functools.partial(plane_kernel, rows_count=rows, steps=steps),
+        grid=(steps,),
+        out_shape=[
+            jax.ShapeDtypeStruct((used, 2, half, LANES), F32),
+            jax.ShapeDtypeStruct((rows, 5, 2, half, LANES), F32),
+        ],
         in_specs=[coef_spec] * 2 + [whole(w.shape) for w in weights],
-        out_specs=pl.BlockSpec((5 * count, 2, 8, LANES), lambda i: (0, 0, i, 0)),
-        scratch_shapes=[pltpu.VMEM((2 * stream_local * 16, LANES), F32)],
-        compiler_params=params(),
+        out_specs=[
+            pl.BlockSpec((used, 2, 8, LANES), lambda i: (0, 0, i, 0)),
+            pl.BlockSpec(memory_space=pl.ANY),
+        ],
+        scratch_shapes=[
+            pltpu.VMEM((2 * stream_local * 16, LANES), F32),
+            pltpu.VMEM((rows, 5, 2, half, LANES), F32),
+            pltpu.SemaphoreType.DMA((steps, rows - 1)),
+            pltpu.SemaphoreType.DMA((steps, rows - 1)),
+            pltpu.SemaphoreType.DMA,
+        ],
+        compiler_params=params(collective_id=0, has_side_effects=True),
         name="plane_values",
     )(v_coef, vort_coef, *weights)
     values = values.reshape(5, count, 2, half, LANES)
@@ -461,7 +518,8 @@
     state = [values] * chunks
     after = [span_inverse, stream_products, span_forward, lambda home: home]
     axes = ["row", "col", "col", "row"]
-    for turn in range(chunks + 3):
+    state[0] = span_inverse(held)
+    for turn in range(1, chunks + 3):
         active = [c for c in range(chunks) if 0 <= turn - c < 4]
         jobs = [(axes[turn - c], c if turn == c else None) for c in active]
         results = exchange(jobs, [state[c] for c in active], sizes, turn)

time: 414 us -> 390 us (0.942)
  Pallas kernels: 375 us -> 352 us
    pallas_call x6 -> x5, Pallas kernels: 272 us -> 226 us  [exchange(): pl.pallas_call(functools.partial(exchange_kernel, jobs=tuple(jobs), sizes...]
    pallas_call x1, Pallas kernels: 28 us -> 50.7 us  [per_device_fast(): pl.pallas_call(functools.partial(plane_kernel, rows_count=rows, steps=ste...]
    unnamed x74 -> x72, local copies, waits for them, and re-layouts: 32.2 us -> 31.7 us
where the time goes in v3:
time: 390 us; the launch traced here: 389 us
  Pallas kernels  352 us (90%)
  local copies, waits for them, and re-layouts  36 us (9%)
    pallas_call x5, Pallas kernels, exchange(): pl.pallas_call(functools.partial(exchange_kernel, jobs=tuple(jobs), sizes...  226 us
    pallas_call x1, Pallas kernels, per_device_fast(): pl.pallas_call(functools.partial(plane_kernel, rows_count=rows, steps=ste...  50.7 us
    unnamed x72, local copies, waits for them, and re-layouts  31.7 us
    pallas_call x1, Pallas kernels, per_device_fast(): pl.pallas_call(functools.partial(combine_kernel, chunks=chunks, rows=rows...  23.6 us
    pallas_call x3, Pallas kernels, stream_products(): pl.pallas_call(stream_kernel, grid=(2 * step // block,), out_shape=jax.Sh...  23 us
    pallas_call x3, Pallas kernels, span_inverse(): pl.pallas_call(functools.partial(span_inverse_kernel, rows=rows, half=hal...  18.9 us
    pallas_call x3, Pallas kernels, span_forward(): pl.pallas_call(span_forward_kernel, out_shape=jax.ShapeDtypeStruct((rows,...  9.3 us

profile of v3, /device:TPU:8, one launch (start us, length us, event | category | flops | bytes accessed | tf_op | source)
XLA Modules:
  0.0 389.1 jit_solution(436066170921576731)
XLA Ops:
  0.7 0.1 fusion.18
  0.8 0.8 fusion.25
  1.6 0.8 slice.9
  2.4 0.8 reshape.152
  3.2 0.7 pad.35.refs_5_
  3.9 0.1 copy.15
  4.1 0.7 broadcast_in_dim.2.refs_4_
  4.8 0.1 copy.16
  4.9 0.1 pad.30
  5.0 0.1 fusion.13
  5.1 0.0 copy-start.35
  5.1 0.0 copy-start.1
  5.1 50.7 %plane_values.1 = (f32[60,2,96,128]{3,2,1,0:T(8,128)S(1)}, f32[4,5,2,96,128]{4,3,2,1,0:T(8,128)S(1)}) custom-call(f32[2,64,192,256]{3,2,1,0:T(8,128)} %v_ref.1, f32[2,64,192,256]{3,2,1,0:T(8,128)} %g_ref.1, bf16[512,128]{1,0:T(8,128)(2,1)S(1)} %get-tuple-element.27.first_ref, bf16[512,128]{1,0:T(8,128)(2,1)S(1)} %get-tuple-element.26.second_ref), custom_call_target="tpu_custom_call" | custom-call | tf_op jit(solution)/shard_map/plane_values/pallas_call | solution.py:453
  55.9 0.0 copy-start.3
  55.9 2.6 copy-done.3
  58.5 0.0 copy-done.35
  58.5 0.2 jit_solution_.3.kz_ref
  58.6 0.0 copy-done.1
  58.7 6.2 %span_inverse.3.refs_0_ = f32[8,6,144,128]{3,2,1,0:T(8,128)S(1)} custom-call(f32[4,5,2,96,128]{4,3,2,1,0:T(8,128)S(1)} %get-tuple-element.14.r_ref, f32[1,128]{1,0:T(1,128)S(1)} %fusion.23.kx_ref.refs_3_, f32[4,2,96,128]{3,2,1,0:T(8,128)S(1)} %jit_solution_.3.kz_ref, bf16[2,2,576,768]{3,2,1,0:T(8,128)(2,1)S(1)} %copy-done.1), custom_call_target="tpu_custom_call" | custom-call | tf_op jit(solution)/shard_map/span_inverse/pallas_call | solution.py:478
  64.9 0.0 copy-start.12
  64.9 1.8 copy-done.12
  66.7 0.7 copy-done.16
  67.4 47.5 %exchange_1.1 = (f32[8,6,144,128]{3,2,1,0:T(8,128)}, f32[4,5,2,96,128]{4,3,2,1,0:T(8,128)}) custom-call(f32[8,6,144,128]{3,2,1,0:T(8,128)} %copy-done.12, f32[5,12,2,96,128]{4,3,2,1,0:T(8,128)} %bitcast.15), custom_call_target="tpu_custom_call" | custom-call | tf_op jit(solution)/shard_map/exchange_1/pallas_call | solution.py:376
  115.0 0.0 copy-start.4
  115.0 1.4 copy-done.4
  116.4 1.4 copy-done.7
  117.8 2.0 copy-done.25
  119.8 7.6 %stream_products.3.refs_0_ = f32[8,3,144,128]{3,2,1,0:T(8,128)S(1)} custom-call(f32[8,6,144,128]{3,2,1,0:T(8,128)S(1)} %copy-done.25, bf16[2,4,256,384]{3,2,1,0:T(8,128)(2,1)S(1)} %copy-done.7, bf16[2,4,384,256]{3,2,1,0:T(8,128)(2,1)S(1)} %copy-done.4), custom_call_target="tpu_custom_call" | custom-call | tf_op jit(solution)/shard_map/stream_products/pallas_call | solution.py:496
  127.5 1.2 copy-done.15
  128.7 6.4 %span_inverse.4.refs_1_ = f32[8,6,144,128]{3,2,1,0:T(8,128)S(1)} custom-call(f32[4,5,2,96,128]{4,3,2,1,0:T(8,128)S(1)} %copy-done.27, f32[1,128]{1,0:T(1,128)S(1)} %fusion.23.kx_ref.refs_3_, f32[4,2,96,128]{3,2,1,0:T(8,128)S(1)} %copy-done.17, bf16[2,2,576,768]{3,2,1,0:T(8,128)(2,1)S(1)} %copy-done.1), custom_call_target="tpu_custom_call" | custom-call | tf_op jit(solution)/shard_map/span_inverse/pallas_call | solution.py:478
  135.1 0.0 copy-start.11
  135.1 1.8 copy-done.11
  136.9 58.8 %exchange_2.1 = (f32[8,3,144,128]{3,2,1,0:T(8,128)}, f32[8,6,144,128]{3,2,1,0:T(8,128)}, f32[4,5,2,96,128]{4,3,2,1,0:T(8,128)}) custom-call(f32[8,3,144,128]{3,2,1,0:T(8,128)} %copy-done.15, f32[8,6,144,128]{3,2,1,0:T(8,128)} %copy-done.11, f32[5,12,2,96,128]{4,3,2,1,0:T(8,128)} %bitcast.16), custom_call_target="tpu_custom_call" | custom-call | tf_op jit(solution)/shard_map/exchange_2/pallas_call | solution.py:376
  195.7 0.0 copy-done
  195.7 0.0 copy-start.28
  195.7 1.5 copy-done.28
  197.2 3.1 span_forward.3.refs_0_
  200.3 1.0 copy-done.19
  201.3 2.0 copy-done.24
  203.4 7.8 %stream_products.4.refs_1_ = f32[8,3,144,128]{3,2,1,0:T(8,128)S(1)} custom-call(f32[8,6,144,128]{3,2,1,0:T(8,128)S(1)} %copy-done.24, bf16[2,4,256,384]{3,2,1,0:T(8,128)(2,1)S(1)} %copy-done.8, bf16[2,4,384,256]{3,2,1,0:T(8,128)(2,1)S(1)} %copy-done.5), custom_call_target="tpu_custom_call" | custom-call | tf_op jit(solution)/shard_map/stream_products/pallas_call | solution.py:496
  211.1 0.0 copy-start.13
  211.2 1.2 copy-done.13
  212.4 6.2 %span_inverse.5.refs_2_ = f32[8,6,144,128]{3,2,1,0:T(8,128)S(1)} custom-call(f32[4,5,2,96,128]{4,3,2,1,0:T(8,128)S(1)} %copy-done.26, f32[1,128]{1,0:T(1,128)S(1)} %fusion.23.kx_ref.refs_3_, f32[4,2,96,128]{3,2,1,0:T(8,128)S(1)} %copy-done.18, bf16[2,2,576,768]{3,2,1,0:T(8,128)(2,1)S(1)} %copy-done.2), custom_call_target="tpu_custom_call" | custom-call | tf_op jit(solution)/shard_map/span_inverse/pallas_call | solution.py:478
  218.6 0.0 copy-start.10
  218.6 1.8 copy-done.10
  220.4 60.9 %exchange_3.1 = (f32[4,3,2,96,128]{4,3,2,1,0:T(8,128)}, f32[8,3,144,128]{3,2,1,0:T(8,128)}, f32[8,6,144,128]{3,2,1,0:T(8,128)}) custom-call(f32[4,3,2,96,128]{4,3,2,1,0:T(8,128)} %copy-done.19, f32[8,3,144,128]{3,2,1,0:T(8,128)} %copy-done.13, f32[8,6,144,128]{3,2,1,0:T(8,128)} %copy-done.10), custom_call_target="tpu_custom_call" | custom-call | tf_op jit(solution)/shard_map/exchange_3/pallas_call | solution.py:376
  281.3 1.5 copy-done.29
  282.8 3.1 span_forward.4.refs_0_
  285.9 0.0 copy-start.21
  285.9 1.0 copy-done.21
  286.9 2.0 copy-done.23
  288.9 7.6 %stream_products.5.refs_1_ = f32[8,3,144,128]{3,2,1,0:T(8,128)S(1)} custom-call(f32[8,6,144,128]{3,2,1,0:T(8,128)S(1)} %copy-done.23, bf16[2,4,256,384]{3,2,1,0:T(8,128)(2,1)S(1)} %copy-done.9, bf16[2,4,384,256]{3,2,1,0:T(8,128)(2,1)S(1)} %copy-done.6), custom_call_target="tpu_custom_call" | custom-call | tf_op jit(solution)/shard_map/stream_products/pallas_call | solution.py:496
  296.6 0.0 copy-start.14
  296.6 1.2 copy-done.14
  297.8 30.4 %exchange_4.1 = (f32[4,3,2,96,128]{4,3,2,1,0:T(8,128)}, f32[8,3,144,128]{3,2,1,0:T(8,128)}) custom-call(f32[4,3,2,96,128]{4,3,2,1,0:T(8,128)} %copy-done.21, f32[8,3,144,128]{3,2,1,0:T(8,128)} %copy-done.14), custom_call_target="tpu_custom_call" | custom-call | tf_op jit(solution)/shard_map/exchange_4/pallas_call | solution.py:376
  328.2 1.5 copy-done.30
  329.7 3.1 span_forward.5.refs_0_
  332.8 0.0 copy-start.20
  332.8 1.0 copy-done.20
  333.8 28.6 %exchange_5.1.refs_2_ = f32[4,3,2,96,128]{4,3,2,1,0:T(8,128)} custom-call(f32[4,3,2,96,128]{4,3,2,1,0:T(8,128)} %copy-done.20), custom_call_target="tpu_custom_call" | custom-call | tf_op jit(solution)/shard_map/exchange_5/pallas_call | solution.py:376
  362.5 1.3 copy-done.22
  363.7 0.9 copy-done.33
  364.6 0.9 copy-done.34
  365.5 23.6 %combinations.1 = (f32[2,64,192,256]{3,2,1,0:T(8,128)}, f32[2,64,192,256]{3,2,1,0:T(8,128)}) custom-call(f32[4,3,2,96,128]{4,3,2,1,0:T(8,128)S(1)} %copy-done.31, f32[4,3,2,96,128]{4,3,2,1,0:T(8,128)S(1)} %copy-done.32, f32[4,3,2,96,128]{4,3,2,1,0:T(8,128)S(1)} %copy-done.22, f32[1,128]{1,0:T(1,128)S(1)} %fusion.23.kx_ref.refs_3_, ...), custom_call_target="tpu_custom_call" | custom-call | tf_op jit(solution)/shard_map/combinations/pallas_call | solution.py:543
  (46 shorter events, 0.2 us)
Async XLA Ops:
  5.1 53.4 %copy-start.35 = (f32[4,2,96]{2,1,0:T(2,128)S(1)}, f32[4,2,96]{2,1,0:T(2,128)}, u32[]{:S(2)}) copy-start(f32[4,2,96]{2,1,0:T(2,128)} %constant.80.clone) | copy-start | bytes 9220
  5.1 53.5 %copy-start.1 = (bf16[2,2,576,768]{3,2,1,0:T(8,128)(2,1)S(1)}, bf16[2,2,576,768]{3,2,1,0:T(8,128)(2,1)}, u32[]{:S(2)}) copy-start(bf16[2,2,576,768]{3,2,1,0:T(8,128)(2,1)} %constant.81.clone.t_ref) | copy-start | bytes 10616836
  55.9 2.6 copy-start.3
  64.9 1.8 copy-start.12
  66.7 0.8 copy-start.16
  115.0 1.4 copy-start.4
  116.4 1.4 copy-start.7
  117.8 2.0 copy-start.25
  119.8 8.9 %copy-start.17 = (f32[4,2,96,128]{3,2,1,0:T(8,128)S(1)}, f32[4,2,96,128]{3,2,1,0:T(8,128)}, u32[]{:S(2)}) copy-start(f32[4,2,96,128]{3,2,1,0:T(8,128)} %copy-done.16) | copy-start | bytes 1179652
  119.8 8.9 %copy-start.27 = (f32[4,5,2,96,128]{4,3,2,1,0:T(8,128)S(1)}, f32[4,5,2,96,128]{4,3,2,1,0:T(8,128)}, u32[]{:S(2)}) copy-start(f32[4,5,2,96,128]{4,3,2,1,0:T(8,128)} %get-tuple-element.17.r_ref) | copy-start | bytes 5898244
  127.4 1.2 copy-start.15
  135.1 1.8 copy-start.11
  136.9 58.9 %copy-start = (bf16[2,2,384,1152]{3,2,1,0:T(8,128)(2,1)S(1)}, bf16[2,2,384,1152]{3,2,1,0:T(8,128)(2,1)}, u32[]{:S(2)}) copy-start(bf16[2,2,384,1152]{3,2,1,0:T(8,128)(2,1)} %constant.84.clone.t_ref) | copy-start | bytes 10616836
  195.7 1.5 copy-start.28
  197.2 4.1 %copy-start.5 = (bf16[2,4,384,256]{3,2,1,0:T(8,128)(2,1)S(1)}, bf16[2,4,384,256]{3,2,1,0:T(8,128)(2,1)}, u32[]{:S(2)}) copy-start(bf16[2,4,384,256]{3,2,1,0:T(8,128)(2,1)} %constant.83.clone.tf_ref) | copy-start | bytes 4718596
  197.2 4.1 %copy-start.8 = (bf16[2,4,256,384]{3,2,1,0:T(8,128)(2,1)S(1)}, bf16[2,4,256,384]{3,2,1,0:T(8,128)(2,1)}, u32[]{:S(2)}) copy-start(bf16[2,4,256,384]{3,2,1,0:T(8,128)(2,1)} %constant.82.clone.ti_ref) | copy-start | bytes 4718596
  200.3 1.0 copy-start.19
  201.3 2.0 copy-start.24
  203.3 9.0 %copy-start.2 = (bf16[2,2,576,768]{3,2,1,0:T(8,128)(2,1)S(1)}, bf16[2,2,576,768]{3,2,1,0:T(8,128)(2,1)}, u32[]{:S(2)}) copy-start(bf16[2,2,576,768]{3,2,1,0:T(8,128)(2,1)} %constant.81.clone.t_ref) | copy-start | bytes 10616836
  203.3 9.0 %copy-start.18 = (f32[4,2,96,128]{3,2,1,0:T(8,128)S(1)}, f32[4,2,96,128]{3,2,1,0:T(8,128)}, u32[]{:S(2)}) copy-start(f32[4,2,96,128]{3,2,1,0:T(8,128)} %copy-done.16) | copy-start | bytes 1179652
  203.3 9.0 %copy-start.26 = (f32[4,5,2,96,128]{4,3,2,1,0:T(8,128)S(1)}, f32[4,5,2,96,128]{4,3,2,1,0:T(8,128)}, u32[]{:S(2)}) copy-start(f32[4,5,2,96,128]{4,3,2,1,0:T(8,128)} %get-tuple-element.20.r_ref) | copy-start | bytes 5898244
  211.1 1.2 copy-start.13
  218.6 1.8 copy-start.10
  281.3 1.5 copy-start.29
  282.8 4.1 %copy-start.6 = (bf16[2,4,384,256]{3,2,1,0:T(8,128)(2,1)S(1)}, bf16[2,4,384,256]{3,2,1,0:T(8,128)(2,1)}, u32[]{:S(2)}) copy-start(bf16[2,4,384,256]{3,2,1,0:T(8,128)(2,1)} %constant.83.clone.tf_ref) | copy-start | bytes 4718596
  282.8 4.1 %copy-start.9 = (bf16[2,4,256,384]{3,2,1,0:T(8,128)(2,1)S(1)}, bf16[2,4,256,384]{3,2,1,0:T(8,128)(2,1)}, u32[]{:S(2)}) copy-start(bf16[2,4,256,384]{3,2,1,0:T(8,128)(2,1)} %constant.82.clone.ti_ref) | copy-start | bytes 4718596
  285.9 1.0 copy-start.21
  286.9 2.0 copy-start.23
  296.6 1.2 copy-start.14
  328.2 1.5 copy-start.30
  332.8 1.0 copy-start.20
  333.8 28.6 %copy-start.31 = (f32[4,3,2,96,128]{4,3,2,1,0:T(8,128)S(1)}, f32[4,3,2,96,128]{4,3,2,1,0:T(8,128)}, u32[]{:S(2)}) copy-start(f32[4,3,2,96,128]{4,3,2,1,0:T(8,128)} %get-tuple-element.21.refs_0_) | copy-start | bytes 3538948
  333.8 28.6 %copy-start.32 = (f32[4,3,2,96,128]{4,3,2,1,0:T(8,128)S(1)}, f32[4,3,2,96,128]{4,3,2,1,0:T(8,128)}, u32[]{:S(2)}) copy-start(f32[4,3,2,96,128]{4,3,2,1,0:T(8,128)} %get-tuple-element.24.refs_1_) | copy-start | bytes 3538948
  362.4 1.3 copy-start.22
  363.7 0.9 copy-start.33
  364.6 0.9 copy-start.34
